TPU v7x, 128 devices: a whole 4x4x4 slice. The times are simulated.
128 devices in a mesh: dp: 8 (over y_lo, x), ctx: 16 (over z, y_hi, core).
Axes of the slice: x: 4, y: 4 (y_hi: 2, y_lo: 2; y = y_hi * 2 + y_lo), z: 4, core: 2. Of those that a mesh axis runs over, the one named last changes fastest.
Arguments:
- query_one: bfloat16 [16384, 4096], P(('dp', 'ctx')), parts along dimension 0, may hold values from -64 to 64
- query_two: bfloat16 [16384, 4096], P(('dp', 'ctx')), parts along dimension 0, may hold values from -64 to 64
- shared_keys: bfloat16 [16384, 512], P(('dp', 'ctx')), parts along dimension 0, may hold values from -8 to 8
- common_values: bfloat16 [16384, 512], P(('dp', 'ctx')), parts along dimension 0, may hold values from -6 to 6
- cotangent_one: bfloat16 [16384, 4096], P(('dp', 'ctx')), parts along dimension 0, may hold values from -96 to 96
- cotangent_two: bfloat16 [16384, 4096], P(('dp', 'ctx')), parts along dimension 0, may hold values from -96 to 96
- span_order: int32 [256], P('dp'), parts along dimension 0, may hold values from 0 to 31, each once
- lengths: int32 [64], P('dp'), parts along dimension 0, may hold values from 1 to 1024, 2048 in all
Outputs:
- query_grad_one: bfloat16 [16384, 4096], P(('dp', 'ctx')), parts along dimension 0
- query_grad_two: bfloat16 [16384, 4096], P(('dp', 'ctx')), parts along dimension 0
- key_grad: bfloat16 [16384, 512], P(('dp', 'ctx')), parts along dimension 0
- value_grad: bfloat16 [16384, 512], P(('dp', 'ctx')), parts along dimension 0
There are 8 independent parts, one for each index of `dp`. A program takes and returns all parts, laid end to end along the dimension named above; each array names one. Nothing has to cross between parts.
Inputs may be any that keep to these rules, and one draw needn't show every extreme that they name: `span_order`: a permutation. `lengths`: they sum to 2048; the largest is exactly 1024.
All inputs are finite; a program needn't handle non-finite values.
Results may differ from a plain program's by a relative error of at most 0.0075.
Values may be sent and summed in bfloat16 or wider, within the bound.
No kernel may reach another device: no remote copies, remote signals or barrier semaphores. Data moves between devices by JAX's collectives and lax.ppermute only.
A program may use at most 320 MiB of HBM per device.

v0:
```python
import jax
import jax.numpy as jnp
from jax import lax
from jax.sharding import PartitionSpec as P

HEAD_SIZE = 128
KEY_VALUE_HEADS = 4
QUERY_PER_KEY = 8
HALF = 64


def head_group(group_width, queries, key_rows, values, cotangent, visible):
    scale = HEAD_SIZE ** (-0.5)
    rows_here = queries.shape[0]
    query_block = queries[
        :, group_width * QUERY_PER_KEY * HEAD_SIZE : (group_width + 1) * QUERY_PER_KEY * HEAD_SIZE
    ].reshape(rows_here, QUERY_PER_KEY, HEAD_SIZE)
    cot_block = cotangent[
        :, group_width * QUERY_PER_KEY * HEAD_SIZE : (group_width + 1) * QUERY_PER_KEY * HEAD_SIZE
    ].reshape(rows_here, QUERY_PER_KEY, HEAD_SIZE)
    key_block = key_rows[:, group_width * HEAD_SIZE : (group_width + 1) * HEAD_SIZE]
    value_block = values[:, group_width * HEAD_SIZE : (group_width + 1) * HEAD_SIZE]
    scores = (
        jnp.einsum("thd,kd->htk", query_block, key_block, preferred_element_type=jnp.float32)
        * scale
    )
    scores = jnp.where(visible[None], scores, -1e30)
    peak = jnp.max(scores, axis=-1, keepdims=True)
    expo = jnp.exp(scores - peak)
    probs = expo / jnp.sum(expo, axis=-1, keepdims=True)
    probs_low = probs.astype(jnp.bfloat16)
    dprobs = jnp.einsum("thd,kd->htk", cot_block, value_block, preferred_element_type=jnp.float32)
    dsum = jnp.sum(probs * dprobs, axis=-1, keepdims=True)
    dscores_low = (probs * (dprobs - dsum) * scale).astype(jnp.bfloat16)
    query_part = jnp.einsum(
        "htk,kd->thd", dscores_low, key_block, preferred_element_type=jnp.float32
    ).reshape(rows_here, QUERY_PER_KEY * HEAD_SIZE)
    key_part = jnp.einsum(
        "htk,thd->kd", dscores_low, query_block, preferred_element_type=jnp.float32
    )
    value_part = jnp.einsum("htk,thd->kd", probs_low, cot_block, preferred_element_type=jnp.float32)
    return (query_part, key_part, value_part)


def layer_grads(queries, key_rows, values, cotangent, visible):
    query_parts, key_parts, value_parts = ([], [], [])
    for group_width in range(KEY_VALUE_HEADS):
        query_part, key_part, value_part = head_group(
            group_width, queries, key_rows, values, cotangent, visible
        )
        query_parts.append(query_part)
        key_parts.append(key_part)
        value_parts.append(value_part)
    return (
        jnp.concatenate(query_parts, axis=1),
        jnp.concatenate(key_parts, axis=1),
        jnp.concatenate(value_parts, axis=1),
    )


def local(
    query_one,
    query_two,
    shared_keys,
    common_values,
    cotangent_one,
    cotangent_two,
    span_order,
    lengths,
):
    all_keys, all_values = (
        lax.all_gather(shared_keys, "ctx", axis=0, tiled=True),
        lax.all_gather(common_values, "ctx", axis=0, tiled=True),
    )
    rows_here = query_one.shape[0]
    total_rows = all_keys.shape[0]
    device_index = lax.axis_index("ctx")
    rows = jnp.arange(total_rows, dtype=jnp.int32)
    slots = jnp.arange(span_order.shape[0], dtype=jnp.int32)
    one_hot = ((rows // HALF)[:, None] == slots[None, :]).astype(jnp.int32)
    positions = jnp.sum(one_hot * span_order[None, :], axis=1) * HALF + rows % HALF
    ends = jnp.cumsum(lengths)
    documents = jnp.sum((positions[:, None] >= ends[None, :]).astype(jnp.int32), axis=1)
    start_row = device_index * rows_here
    local_pos = lax.dynamic_slice_in_dim(positions, start_row, rows_here)
    local_doc = lax.dynamic_slice_in_dim(documents, start_row, rows_here)
    visible = (positions[None, :] <= local_pos[:, None]) & (
        documents[None, :] == local_doc[:, None]
    )
    grad_q1, grad_k1, grad_v1 = layer_grads(query_one, all_keys, all_values, cotangent_one, visible)
    grad_q2, grad_k2, grad_v2 = layer_grads(query_two, all_keys, all_values, cotangent_two, visible)
    width = grad_k1.shape[1]
    stacked = jnp.concatenate([grad_k1 + grad_k2, grad_v1 + grad_v2], axis=1)
    summed = lax.psum_scatter(stacked, "ctx", scatter_dimension=0, tiled=True)
    key_sum = summed[:, :width]
    value_sum = summed[:, width:]
    return (
        grad_q1.astype(jnp.bfloat16),
        grad_q2.astype(jnp.bfloat16),
        key_sum.astype(jnp.bfloat16),
        value_sum.astype(jnp.bfloat16),
    )


def solution(mesh):
    in_specs = (
        P(("dp", "ctx"), None),
        P(("dp", "ctx"), None),
        P(("dp", "ctx"), None),
        P(("dp", "ctx"), None),
        P(("dp", "ctx"), None),
        P(("dp", "ctx"), None),
        P("dp"),
        P("dp"),
    )
    out_specs = (
        P(("dp", "ctx"), None),
        P(("dp", "ctx"), None),
        P(("dp", "ctx"), None),
        P(("dp", "ctx"), None),
    )
    return jax.shard_map(local, mesh=mesh, in_specs=in_specs, out_specs=out_specs, check_vma=False)
```

profile of v0, /device:TPU:13, one launch (start us, length us, event | category | flops | bytes accessed | tf_op | source)
XLA Modules:
  0.0 490.0 jit_solution(15425951806183071014)
XLA Ops:
  24.2 35.7 %all-gather.3.cloned.1.call-done = bf16[2048,512]{1,0:T(8,128)(2,1)} async-done(((bf16[128,512]{1,0:T(8,128)(2,1)}), bf16[2048,512]{1,0:T(8,128)(2,1)}) %all-gather.3.cloned.1.call-update) | async-done | bytes 2097168 | tf_op jit(solution)/shard_map/all_gather | solution.py:72
  59.9 7.1 %fusion.241 = (f32[8,128]{1,0:T(8,128)S(1)}, f32[8,128,2048]{1,2,0:T(8,128)}) fusion(pred[128,2048]{0,1:T(8,128)(4,1)S(1)} %compare_and_fusion, bf16[128,8,128]{0,2,1:T(8,128)(2,1)} %bitcast.560, bf16[2048,512]{1,0:T(8,128)(2,1)} %all-gather.3.cloned.1.call-done), kind=kOutput, calls=%fused_computation.278 | convolution fusion | flops 545261568 | bytes 9441280 | tf_op jit(solution)/shard_map/sub | solution.py:29
  72.9 35.9 %all-gather.5.cloned.1.call-done = bf16[2048,512]{1,0:T(8,128)(2,1)} async-done(((bf16[128,512]{1,0:T(8,128)(2,1)}), bf16[2048,512]{1,0:T(8,128)(2,1)}) %all-gather.5.cloned.1.call-update) | async-done | bytes 2097168 | tf_op jit(solution)/shard_map/all_gather | solution.py:73
  114.3 14.5 %fusion.112 = f32[2048,128]{0,1:T(8,128)} fusion(bf16[128,8,128]{0,2,1:T(8,128)(2,1)S(1)} %bitcast.561, f32[2048,128,8]{1,0,2:T(8,128)} %fusion.174, f32[8,128,2048]{1,2,0:T(8,128)} %get-tuple-element.43, f32[8,128]{1,0:T(8,128)S(1)} %get-tuple-element.42), kind=kOutput, calls=%fused_computation.155 | convolution fusion | flops 551554048 | bytes 18092032 | tf_op jit(solution)/shard_map/htk,thd->kd/dot_general | solution.py:38
  146.3 14.2 %fusion.114 = f32[2048,128]{0,1:T(8,128)} fusion(bf16[128,8,128]{0,2,1:T(8,128)(2,1)} %bitcast.558, f32[2048,128,8]{1,0,2:T(8,128)} %fusion.170, f32[8,128,2048]{1,2,0:T(8,128)} %get-tuple-element.47, f32[8,128]{1,0:T(8,128)S(1)} %get-tuple-element.46), kind=kOutput, calls=%fused_computation.157 | convolution fusion | flops 551554048 | bytes 18092032 | tf_op jit(solution)/shard_map/htk,thd->kd/dot_general | solution.py:38
  160.4 7.1 %fusion.242 = (f32[8,128]{1,0:T(8,128)S(1)}, f32[8,128,2048]{1,2,0:T(8,128)}) fusion(pred[128,2048]{0,1:T(8,128)(4,1)S(1)} %copy-done.13, bf16[128,8,128]{0,2,1:T(8,128)(2,1)} %bitcast.556, bf16[2048,512]{1,0:T(8,128)(2,1)} %all-gather.3.cloned.1.call-done), kind=kOutput, calls=%fused_computation.279 | convolution fusion | flops 545261568 | bytes 9441280 | tf_op jit(solution)/shard_map/sub | solution.py:29
  178.1 14.2 %fusion.113 = f32[2048,128]{0,1:T(8,128)} fusion(bf16[128,8,128]{0,2,1:T(8,128)(2,1)} %bitcast.557, f32[2048,128,8]{1,0,2:T(8,128)} %fusion.172, f32[8,128,2048]{1,2,0:T(8,128)} %get-tuple-element.45, f32[8,128]{1,0:T(8,128)S(1)} %get-tuple-element.44), kind=kOutput, calls=%fused_computation.156 | convolution fusion | flops 551554048 | bytes 18092032 | tf_op jit(solution)/shard_map/htk,thd->kd/dot_general | solution.py:38
  209.6 14.8 %fusion.115 = f32[2048,128]{0,1:T(8,128)} fusion(bf16[128,8,128]{0,2,1:T(8,128)(2,1)S(1)} %bitcast.555, f32[2048,128,8]{1,0,2:T(8,128)} %fusion.168, f32[8,128,2048]{1,2,0:T(8,128)} %get-tuple-element.49, f32[8,128]{1,0:T(8,128)S(1)} %get-tuple-element.48), kind=kOutput, calls=%fused_computation.158 | convolution fusion | flops 551554048 | bytes 18092032 | tf_op jit(solution)/shard_map/htk,thd->kd/dot_general | solution.py:38
  241.8 14.4 %fusion.116 = f32[2048,128]{0,1:T(8,128)} fusion(bf16[128,8,128]{0,2,1:T(8,128)(2,1)S(1)} %bitcast.553, f32[2048,128,8]{1,0,2:T(8,128)} %fusion.175, f32[8,128,2048]{1,2,0:T(8,128)} %get-tuple-element.35, f32[8,128]{1,0:T(8,128)S(1)} %get-tuple-element.34), kind=kOutput, calls=%fused_computation.159 | convolution fusion | flops 551554048 | bytes 18092032 | tf_op jit(solution)/shard_map/htk,thd->kd/dot_general | solution.py:38
  256.1 7.0 %fusion.239 = (f32[8,128]{1,0:T(8,128)S(1)}, f32[8,128,2048]{1,2,0:T(8,128)}) fusion(pred[128,2048]{0,1:T(8,128)(4,1)S(1)} %copy-done.13, bf16[128,8,128]{0,2,1:T(8,128)(2,1)S(1)} %bitcast.550, bf16[2048,512]{1,0:T(8,128)(2,1)} %all-gather.3.cloned.1.call-done), kind=kOutput, calls=%fused_computation.276 | convolution fusion | flops 545261568 | bytes 9441280 | tf_op jit(solution)/shard_map/sub | solution.py:29
  273.6 14.6 %fusion.118 = f32[2048,128]{0,1:T(8,128)} fusion(bf16[128,8,128]{0,2,1:T(8,128)(2,1)S(1)} %bitcast.551, f32[2048,128,8]{1,0,2:T(8,128)} %fusion.171, f32[8,128,2048]{1,2,0:T(8,128)} %get-tuple-element.39, f32[8,128]{1,0:T(8,128)S(1)} %get-tuple-element.38), kind=kOutput, calls=%fused_computation.161 | convolution fusion | flops 551554048 | bytes 18092032 | tf_op jit(solution)/shard_map/htk,thd->kd/dot_general | solution.py:38
  288.2 7.1 %fusion.238 = (f32[8,128]{1,0:T(8,128)S(1)}, f32[8,128,2048]{1,2,0:T(8,128)}) fusion(pred[128,2048]{0,1:T(8,128)(4,1)S(1)} %copy-done.13, bf16[128,8,128]{0,2,1:T(8,128)(2,1)S(1)} %bitcast.548, bf16[2048,512]{1,0:T(8,128)(2,1)} %all-gather.3.cloned.1.call-done), kind=kOutput, calls=%fused_computation.275 | convolution fusion | flops 545261568 | bytes 9441280 | tf_op jit(solution)/shard_map/sub | solution.py:29
  305.7 14.3 %fusion.117 = f32[2048,128]{0,1:T(8,128)} fusion(bf16[128,8,128]{0,2,1:T(8,128)(2,1)S(1)} %bitcast.549, f32[2048,128,8]{1,0,2:T(8,128)} %fusion.173, f32[8,128,2048]{1,2,0:T(8,128)} %get-tuple-element.37, f32[8,128]{1,0:T(8,128)S(1)} %get-tuple-element.36), kind=kOutput, calls=%fused_computation.160 | convolution fusion | flops 551554048 | bytes 18092032 | tf_op jit(solution)/shard_map/htk,thd->kd/dot_general | solution.py:38
  320.0 7.1 %fusion.240 = (f32[8,128]{1,0:T(8,128)S(1)}, f32[8,128,2048]{1,2,0:T(8,128)}) fusion(pred[128,2048]{0,1:T(8,128)(4,1)S(1)} %copy-done.14, bf16[128,8,128]{0,2,1:T(8,128)(2,1)S(1)} %bitcast.546, bf16[2048,512]{1,0:T(8,128)(2,1)} %all-gather.3.cloned.1.call-done), kind=kOutput, calls=%fused_computation.277 | convolution fusion | flops 545261568 | bytes 9441280 | tf_op jit(solution)/shard_map/sub | solution.py:29
  337.5 14.4 %fusion.119 = f32[2048,128]{0,1:T(8,128)} fusion(bf16[128,8,128]{0,2,1:T(8,128)(2,1)S(1)} %bitcast.547, f32[2048,128,8]{1,0,2:T(8,128)} %fusion.169, f32[8,128,2048]{1,2,0:T(8,128)} %get-tuple-element.41, f32[8,128]{1,0:T(8,128)S(1)} %get-tuple-element.40), kind=kOutput, calls=%fused_computation.162 | convolution fusion | flops 551554048 | bytes 18092032 | tf_op jit(solution)/shard_map/htk,thd->kd/dot_general | solution.py:38
  351.8 8.1 %maximum_add_fusion = (f32[2048,512]{0,1:T(8,128)S(1)}, f32[2048,512]{0,1:T(8,128)}) fusion(f32[2048,128]{0,1:T(8,128)} %fusion.116, f32[2048,128]{0,1:T(8,128)} %fusion.117, f32[2048,128]{0,1:T(8,128)} %fusion.118, f32[2048,128]{0,1:T(8,128)} %fusion.119, f32[2048,128]{0,1:T(8,128)S(1)} %copy-done.5, f32[2048,128]{0,1:T(8,128)} %fusion.113, ...), kind=kLoop, calls=%fused_computation.81 | loop fusion | flops 14680064 | bytes 25165824 | tf_op jit(solution)/shard_map/add | solution.py:93
  368.0 14.3 %fusion.144 = bf16[8,128,128]{1,2,0:T(8,128)(2,1)S(1)} fusion(f32[2048,128,8]{1,0,2:T(8,128)} %fusion.174, bf16[2048,512]{1,0:T(8,128)(2,1)S(1)} %copy-done.17, f32[8,128,2048]{1,2,0:T(8,128)} %get-tuple-element.43, f32[8,128]{1,0:T(8,128)S(1)} %copy-done.19), kind=kOutput, calls=%fused_computation.171 | convolution fusion | flops 551685120 | bytes 34349056 | tf_op jit(solution)/shard_map/htk,kd->thd/dot_general | solution.py:35
  382.5 15.1 %fusion.146 = bf16[8,128,128]{1,2,0:T(8,128)(2,1)S(1)} fusion(f32[2048,128,8]{1,0,2:T(8,128)} %fusion.170, bf16[2048,512]{1,0:T(8,128)(2,1)S(1)} %copy-done.17, f32[8,128,2048]{1,2,0:T(8,128)} %get-tuple-element.47, f32[8,128]{1,0:T(8,128)S(1)} %copy-done.21), kind=kOutput, calls=%fused_computation.173 | convolution fusion | flops 551685120 | bytes 34349056 | tf_op jit(solution)/shard_map/htk,kd->thd/dot_general | solution.py:35
  397.9 13.8 %fusion.145 = bf16[8,128,128]{1,2,0:T(8,128)(2,1)S(1)} fusion(f32[2048,128,8]{1,0,2:T(8,128)} %fusion.172, bf16[2048,512]{1,0:T(8,128)(2,1)S(1)} %copy-done.17, f32[8,128,2048]{1,2,0:T(8,128)} %get-tuple-element.45, f32[8,128]{1,0:T(8,128)S(1)} %copy-done.23), kind=kOutput, calls=%fused_computation.172 | convolution fusion | flops 551685120 | bytes 34349056 | tf_op jit(solution)/shard_map/htk,kd->thd/dot_general | solution.py:35
  411.8 13.5 %fusion.147 = bf16[8,128,128]{1,2,0:T(8,128)(2,1)S(1)} fusion(f32[2048,128,8]{1,0,2:T(8,128)} %fusion.168, bf16[2048,512]{1,0:T(8,128)(2,1)S(1)} %copy-done.17, f32[8,128,2048]{1,2,0:T(8,128)} %get-tuple-element.49, f32[8,128]{1,0:T(8,128)S(1)} %copy-done.25), kind=kOutput, calls=%fused_computation.174 | convolution fusion | flops 551685120 | bytes 34349056 | tf_op jit(solution)/shard_map/htk,kd->thd/dot_general | solution.py:35
  425.4 13.5 %fusion.148 = bf16[8,128,128]{1,2,0:T(8,128)(2,1)S(1)} fusion(f32[2048,128,8]{1,0,2:T(8,128)} %fusion.175, bf16[2048,512]{1,0:T(8,128)(2,1)} %all-gather.3.cloned.1.call-done, f32[8,128,2048]{1,2,0:T(8,128)} %get-tuple-element.35, f32[8,128]{1,0:T(8,128)S(1)} %copy-done.27), kind=kOutput, calls=%fused_computation.175 | convolution fusion | flops 551685120 | bytes 34349056 | tf_op jit(solution)/shard_map/htk,kd->thd/dot_general | solution.py:35
  439.1 13.2 %fusion.150 = bf16[8,128,128]{1,2,0:T(8,128)(2,1)S(1)} fusion(f32[2048,128,8]{1,0,2:T(8,128)} %fusion.171, bf16[2048,512]{1,0:T(8,128)(2,1)} %all-gather.3.cloned.1.call-done, f32[8,128,2048]{1,2,0:T(8,128)} %get-tuple-element.39, f32[8,128]{1,0:T(8,128)S(1)} %get-tuple-element.38), kind=kOutput, calls=%fused_computation.177 | convolution fusion | flops 551685120 | bytes 34349056 | tf_op jit(solution)/shard_map/htk,kd->thd/dot_general | solution.py:35
  452.4 13.3 %fusion.149 = bf16[8,128,128]{1,2,0:T(8,128)(2,1)S(1)} fusion(f32[2048,128,8]{1,0,2:T(8,128)} %fusion.173, bf16[2048,512]{1,0:T(8,128)(2,1)} %all-gather.3.cloned.1.call-done, f32[8,128,2048]{1,2,0:T(8,128)} %get-tuple-element.37, f32[8,128]{1,0:T(8,128)S(1)} %get-tuple-element.36), kind=kOutput, calls=%fused_computation.176 | convolution fusion | flops 551685120 | bytes 34349056 | tf_op jit(solution)/shard_map/htk,kd->thd/dot_general | solution.py:35
  465.9 13.1 %fusion.151 = bf16[8,128,128]{1,2,0:T(8,128)(2,1)S(1)} fusion(f32[2048,128,8]{1,0,2:T(8,128)} %fusion.169, bf16[2048,512]{1,0:T(8,128)(2,1)} %all-gather.3.cloned.1.call-done, f32[8,128,2048]{1,2,0:T(8,128)} %get-tuple-element.41, f32[8,128]{1,0:T(8,128)S(1)} %get-tuple-element.40), kind=kOutput, calls=%fused_computation.178 | convolution fusion | flops 551685120 | bytes 34349056 | tf_op jit(solution)/shard_map/htk,kd->thd/dot_general | solution.py:35
  (124 shorter events, 135.5 us)
Async XLA Ops:
  7.2 12.1 %copy-start.6 = (bf16[128,4096]{1,0:T(8,128)(2,1)S(1)}, bf16[128,4096]{1,0:T(8,128)(2,1)}, u32[]{:S(2)}) copy-start(bf16[128,4096]{1,0:T(8,128)(2,1)} %param.12) | copy-start | bytes 3145732
  7.2 14.9 %copy-start.7 = (bf16[128,4096]{1,0:T(8,128)(2,1)S(1)}, bf16[128,4096]{1,0:T(8,128)(2,1)}, u32[]{:S(2)}) copy-start(bf16[128,4096]{1,0:T(8,128)(2,1)} %param.13) | copy-start | bytes 3145732
  7.2 52.7 %all-gather.3.cloned.1.call-start = ((), (), s32[]{:S(2)}) async-start(), calls=%async_computation.1 | async-start | bytes 2228224 | tf_op jit(solution)/shard_map/all_gather | solution.py:72
  7.9 100.9 %all-gather.5.cloned.1.call-start = ((), (), s32[]{:S(2)}) async-start(), calls=%async_computation.2 | async-start | bytes 2228224 | tf_op jit(solution)/shard_map/all_gather | solution.py:73
  8.7 472.0 %reduce-scatter.2.cloned.1.call-start = ((), (), s32[]{:S(2)}) async-start(), calls=%async_computation.3 | async-start | bytes 8912896 | tf_op jit(solution)/shard_map/reduce_scatter | solution.py:94
  24.2 104.6 %copy-start.12 = (pred[128,2048]{0,1:T(8,128)(4,1)}, pred[128,2048]{0,1:T(8,128)(4,1)S(1)}, u32[]{:S(2)}) copy-start(pred[128,2048]{0,1:T(8,128)(4,1)S(1)} %compare_and_fusion) | copy-start | bytes 786436
  67.0 47.2 %copy-start.18 = (f32[8,128]{1,0:T(8,128)}, f32[8,128]{1,0:T(8,128)S(1)}, u32[]{:S(2)}) copy-start(f32[8,128]{1,0:T(8,128)S(1)} %get-tuple-element.42) | copy-start | bytes 12292
  72.9 41.4 %copy-start.16 = (bf16[128,1024]{0,1:T(8,128)(2,1)S(1)}, bf16[128,1024]{0,1:T(8,128)(2,1)}, u32[]{:S(2)}) copy-start(bf16[128,1024]{0,1:T(8,128)(2,1)} %copy.288) | copy-start | bytes 786436
  114.3 14.5 %copy-start.15 = (bf16[128,1024]{0,1:T(8,128)(2,1)S(1)}, bf16[128,1024]{0,1:T(8,128)(2,1)}, u32[]{:S(2)}) copy-start(bf16[128,1024]{0,1:T(8,128)(2,1)} %copy.284) | copy-start | bytes 786436
  135.8 10.5 %copy-start.20 = (f32[8,128]{1,0:T(8,128)}, f32[8,128]{1,0:T(8,128)S(1)}, u32[]{:S(2)}) copy-start(f32[8,128]{1,0:T(8,128)S(1)} %get-tuple-element.46) | copy-start | bytes 12292
  146.3 14.2 %copy-start.13 = (pred[128,2048]{0,1:T(8,128)(4,1)S(1)}, pred[128,2048]{0,1:T(8,128)(4,1)}, u32[]{:S(2)}) copy-start(pred[128,2048]{0,1:T(8,128)(4,1)} %copy-done.12) | copy-start | bytes 786436
  167.5 10.5 %copy-start.22 = (f32[8,128]{1,0:T(8,128)}, f32[8,128]{1,0:T(8,128)S(1)}, u32[]{:S(2)}) copy-start(f32[8,128]{1,0:T(8,128)S(1)} %get-tuple-element.44) | copy-start | bytes 12292
  178.1 14.2 %copy-start.11 = (bf16[128,1024]{0,1:T(8,128)(2,1)S(1)}, bf16[128,1024]{0,1:T(8,128)(2,1)}, u32[]{:S(2)}) copy-start(bf16[128,1024]{0,1:T(8,128)(2,1)} %copy.282) | copy-start | bytes 786436
  231.4 10.4 %copy-start.26 = (f32[8,128]{1,0:T(8,128)}, f32[8,128]{1,0:T(8,128)S(1)}, u32[]{:S(2)}) copy-start(f32[8,128]{1,0:T(8,128)S(1)} %get-tuple-element.34) | copy-start | bytes 12292
  241.8 14.4 %copy-start.10 = (bf16[128,1024]{0,1:T(8,128)(2,1)S(1)}, bf16[128,1024]{0,1:T(8,128)(2,1)}, u32[]{:S(2)}) copy-start(bf16[128,1024]{0,1:T(8,128)(2,1)} %copy.276) | copy-start | bytes 786436
  273.6 14.6 %copy-start.9 = (bf16[128,1024]{0,1:T(8,128)(2,1)S(1)}, bf16[128,1024]{0,1:T(8,128)(2,1)}, u32[]{:S(2)}) copy-start(bf16[128,1024]{0,1:T(8,128)(2,1)} %copy.278) | copy-start | bytes 786436
  305.7 14.3 %copy-start.8 = (bf16[128,1024]{0,1:T(8,128)(2,1)S(1)}, bf16[128,1024]{0,1:T(8,128)(2,1)}, u32[]{:S(2)}) copy-start(bf16[128,1024]{0,1:T(8,128)(2,1)} %copy.274) | copy-start | bytes 786436
  305.7 14.3 %copy-start.14 = (pred[128,2048]{0,1:T(8,128)(4,1)S(1)}, pred[128,2048]{0,1:T(8,128)(4,1)}, u32[]{:S(2)}) copy-start(pred[128,2048]{0,1:T(8,128)(4,1)} %copy-done.12) | copy-start | bytes 786436
  337.4 14.4 %copy-start.4 = (f32[2048,128]{0,1:T(8,128)S(1)}, f32[2048,128]{0,1:T(8,128)}, u32[]{:S(2)}) copy-start(f32[2048,128]{0,1:T(8,128)} %fusion.141) | copy-start | bytes 3145732
  337.4 14.4 %copy-start.5 = (f32[2048,128]{0,1:T(8,128)S(1)}, f32[2048,128]{0,1:T(8,128)}, u32[]{:S(2)}) copy-start(f32[2048,128]{0,1:T(8,128)} %fusion.112) | copy-start | bytes 3145732
  368.0 14.5 %copy-start.21 = (f32[8,128]{1,0:T(8,128)S(1)}, f32[8,128]{1,0:T(8,128)}, u32[]{:S(2)}) copy-start(f32[8,128]{1,0:T(8,128)} %copy-done.20) | copy-start | bytes 12292
  382.5 15.3 %copy-start.23 = (f32[8,128]{1,0:T(8,128)S(1)}, f32[8,128]{1,0:T(8,128)}, u32[]{:S(2)}) copy-start(f32[8,128]{1,0:T(8,128)} %copy-done.22) | copy-start | bytes 12292
  397.8 13.9 %copy-start.25 = (f32[8,128]{1,0:T(8,128)S(1)}, f32[8,128]{1,0:T(8,128)}, u32[]{:S(2)}) copy-start(f32[8,128]{1,0:T(8,128)} %copy-done.24) | copy-start | bytes 12292
  411.8 13.6 %copy-start.27 = (f32[8,128]{1,0:T(8,128)S(1)}, f32[8,128]{1,0:T(8,128)}, u32[]{:S(2)}) copy-start(f32[8,128]{1,0:T(8,128)} %copy-done.26) | copy-start | bytes 12292
  (7 other events, 40.9 us)
Sparse Core Ops, SparseCore 0:
  10.5 49.3 all-gather.2
  62.4 46.3 all-gather.4
  366.6 99.7 reduce-scatter.1
where the time goes:
time: 500 us; the launch traced here: 490 us
  matrix products  366 us (73%)
  waiting for transfers between devices  73 us (15%)
  other arithmetic  20.2 us (4%)
  local copies, waits for them, and re-layouts  16.7 us (3%)
  between operations  14.3 us (3%)
    dot_general x8, matrix products, head_group(): jnp.einsum('htk,thd->kd', dscores_low, query_block, preferred_element_typ...  115 us
    dot_general x8, matrix products, head_group(): jnp.einsum('htk,kd->thd', dscores_low, key_block, preferred_element_type=...  110 us
    sub x8, matrix products, head_group(): expo = jnp.exp(scores - peak)  56.5 us
    dot_general x8, matrix products, head_group(): jnp.einsum('htk,thd->kd', probs_low, cot_block, preferred_element_type=jn...  47.2 us
    dot_general x8, matrix products, head_group(): jnp.einsum('thd,kd->htk', cot_block, value_block, preferred_element_type=...  36.9 us
    all_gather x1, waiting for transfers between devices, local(): lax.all_gather(common_values, 'ctx', axis=0, tiled=True)  35.9 us
    all_gather x1, waiting for transfers between devices, local(): lax.all_gather(shared_keys, 'ctx', axis=0, tiled=True)  35.7 us
    unnamed x74, local copies, waits for them, and re-layouts  12.7 us
  transfers between devices with their start and end apart: 3, of which 2 were waited for; matrix products, arithmetic and copies ran while one was open for 29% of the time, Pallas kernels for 0%

commit v1 on v0

v1 whole, which is shorter than its diff:
```python
import math

import jax
import jax.numpy as jnp
from jax import lax
from jax.experimental import pallas as pl
from jax.experimental.pallas import tpu as pltpu
from jax.sharding import PartitionSpec as P

HEAD = 128
KEY_VALUE_HEADS = 4
QUERY_PER_KEY = 8
HALF = 64
MOST = 1024
NEG = -1e30
SCALE = HEAD**-0.5
LOG2E = math.log2(math.e)
Z, Y = 4, 2
CHIPS = Z * Y
TOKENS = 2048
BLOCKS = TOKENS // HALF
HEADS_HERE = KEY_VALUE_HEADS // 2
WIDTH = QUERY_PER_KEY * HEAD
ROWS = 2 * QUERY_PER_KEY * HALF
TILE = 256
PAD = TILE
STEPS = -(-(MOST + HALF) // TILE)
LANES = 512
CHUNKS = ROWS // LANES
OFFSETS = ((0, 0), (0, 1), (-1, 0), (-1, 1), (1, 0), (1, 1), (-2, 0), (2, 1))


def device_of(z, y, core):
    return ((z % Z) * Y + y % Y) * 2 + core


def moves(dz, dy, dcore):
    return [
        (device_of(z, y, c), device_of(z + dz, y + dy, (c + dcore) % 2))
        for z in range(Z)
        for y in range(Y)
        for c in range(2)
    ]


def send(x, dz, dy, dcore=0):
    return lax.ppermute(x, "ctx", moves(dz, dy, dcore))


def block_grads(position, lens, qs, gs, dqs, ks, vs, dk, dv, es, dps, ms, dqt, qst, gst, bias):
    token = lax.broadcasted_iota(jnp.int32, (1, 128), 1) % HALF
    where = position * HALF + token
    starts = jnp.zeros((1, 128), jnp.int32)
    low = jnp.int32(0)
    end = jnp.int32(0)
    for k in range(lens.shape[0]):
        end = end + lens[k]
        starts = jnp.where(where >= end, end, starts)
        low = jnp.where(position * HALF >= end, end, low)
    stop = (position + 1) * HALF
    steps = (stop - low + TILE - 1) // TILE
    for layer in range(2):
        for h in range(QUERY_PER_KEY):
            r = (layer * QUERY_PER_KEY + h) * HALF
            qst[r : r + HALF, :] = qs[layer][:, h * HEAD : (h + 1) * HEAD]
            gst[r : r + HALF, :] = gs[layer][:, h * HEAD : (h + 1) * HEAD]
    by_head = (((1,), (1,)), ((), ()))

    def scores(t, carry):
        base = stop - (t + 1) * TILE
        row = pl.multiple_of(base + PAD, HALF)
        at = pl.multiple_of(t * TILE, TILE)
        kt = ks[pl.ds(row, TILE), :]
        vt = vs[pl.ds(row, TILE), :]
        key = base + lax.broadcasted_iota(jnp.int32, (TILE, 128), 0)
        bias[...] = jnp.where((key <= where) & (key >= starts), 0.0, NEG)
        out = []
        for c in range(CHUNKS):
            top, total, mean = carry[c]
            sl = slice(c * LANES, (c + 1) * LANES)
            s = lax.dot_general(kt, qst[sl, :], by_head, preferred_element_type=jnp.float32)
            dp = lax.dot_general(vt, gst[sl, :], by_head, preferred_element_type=jnp.float32)
            s = s * (SCALE * LOG2E) + jnp.concatenate([bias[...]] * (LANES // 128), axis=1)
            now = jnp.maximum(top, jnp.max(s, axis=0, keepdims=True))
            e = jnp.exp2(s - now)
            shrink = jnp.exp2(top - now)
            total = total * shrink + jnp.sum(e, axis=0, keepdims=True)
            mean = mean * shrink + jnp.sum(e * dp, axis=0, keepdims=True)
            es[pl.ds(at, TILE), sl] = e
            dps[pl.ds(at, TILE), sl] = dp
            ms[t, :, sl] = jnp.broadcast_to(now, (8, LANES))
            out.append((now, total, mean))
        return tuple(out)

    zero = jnp.zeros((1, LANES), jnp.float32)
    found = lax.fori_loop(0, steps, scores, tuple((zero + NEG, zero, zero) for _ in range(CHUNKS)))
    inverse = [1.0 / f[1] for f in found]
    dsum = [f[2] * i for f, i in zip(found, inverse)]
    dqt[...] = jnp.zeros_like(dqt)

    def grads(t, _):
        row = pl.multiple_of(stop - (t + 1) * TILE + PAD, HALF)
        at = pl.multiple_of(t * TILE, TILE)
        kt = ks[pl.ds(row, TILE), :]
        dvt = dv[pl.ds(row, TILE), :]
        dkt = dk[pl.ds(row, TILE), :]
        for c in range(CHUNKS):
            sl = slice(c * LANES, (c + 1) * LANES)
            p = es[pl.ds(at, TILE), sl] * (jnp.exp2(ms[t, 0:1, sl] - found[c][0]) * inverse[c])
            ds = (p * (dps[pl.ds(at, TILE), sl] - dsum[c]) * SCALE).astype(jnp.bfloat16)
            dvt = dvt + jnp.dot(p.astype(jnp.bfloat16), gst[sl, :], preferred_element_type=jnp.float32)
            dkt = dkt + jnp.dot(ds, qst[sl, :], preferred_element_type=jnp.float32)
            dqt[:, sl] += lax.dot_general(kt, ds, (((0,), (0,)), ((), ())), preferred_element_type=jnp.float32)
        dv[pl.ds(row, TILE), :] = dvt
        dk[pl.ds(row, TILE), :] = dkt
        return 0

    lax.fori_loop(0, steps, grads, 0)
    for layer in range(2):
        for h in range(0, QUERY_PER_KEY, 2):
            r = (layer * QUERY_PER_KEY + h) * HALF
            x = dqt[:, r : r + 128].astype(jnp.bfloat16).T
            dqs[layer][:, h * HEAD : (h + 1) * HEAD] = x[:HALF]
            dqs[layer][:, (h + 1) * HEAD : (h + 2) * HEAD] = x[HALF:]


def kernel(core, table, lens, *refs):
    own, other, pieces, outs, total, scratch = refs[:4], refs[4:8], refs[8:16], refs[16:20], refs[20], refs[21:]
    ks, vs, dk, dv = scratch[:4]
    step = pl.program_id(0)

    @pl.when(step == 0)
    def _():
        ks[:PAD, :] = jnp.zeros((PAD, HEAD), jnp.bfloat16)
        vs[:PAD, :] = jnp.zeros((PAD, HEAD), jnp.bfloat16)
        dk[...] = jnp.zeros_like(dk)
        dv[...] = jnp.zeros_like(dv)
        for i in range(BLOCKS):
            p = pl.multiple_of(table[i] * HALF + PAD, HALF)
            x = pieces[i // 4][(i % 4) * HALF : (i % 4 + 1) * HALF, :]
            ks[pl.ds(p, HALF), :] = x[:, :HEAD]
            vs[pl.ds(p, HALF), :] = x[:, HEAD:]

    block_grads(table[step], lens, own[:2], own[2:], outs[:2], *scratch)
    block_grads(table[step + 2], lens, other[:2], other[2:], outs[2:], *scratch)

    @pl.when(step == 1)
    def _():
        for i in range(BLOCKS):
            p = pl.multiple_of(table[i] * HALF + PAD, HALF)
            rows = slice((i % 4) * HALF, (i % 4 + 1) * HALF)
            total[i // 4, rows, :HEAD] = dk[pl.ds(p, HALF), :].astype(jnp.bfloat16)
            total[i // 4, rows, HEAD:] = dv[pl.ds(p, HALF), :].astype(jnp.bfloat16)


def head_grads(g, core, table, lens, own, other, pieces):
    return pl.pallas_call(
        kernel,
        grid_spec=pltpu.PrefetchScalarGridSpec(
            num_scalar_prefetch=3,
            grid=(2,),
            in_specs=[pl.BlockSpec((HALF, WIDTH), lambda s, core, *_: (s, core[0] * HEADS_HERE + g))] * 4
            + [pl.BlockSpec((HALF, WIDTH), lambda s, *_: (s, g))] * 4
            + [pl.BlockSpec((4 * HALF, 2 * HEAD), lambda s, *_: (0, 0))] * CHIPS,
            out_specs=[pl.BlockSpec((HALF, WIDTH), lambda s, *_: (s, 0))] * 4
            + [pl.BlockSpec((CHIPS, 4 * HALF, 2 * HEAD), lambda s, *_: (0, 0, 0))],
            scratch_shapes=[
                pltpu.VMEM((TOKENS + PAD, HEAD), jnp.bfloat16),
                pltpu.VMEM((TOKENS + PAD, HEAD), jnp.bfloat16),
                pltpu.VMEM((TOKENS + PAD, HEAD), jnp.float32),
                pltpu.VMEM((TOKENS + PAD, HEAD), jnp.float32),
                pltpu.VMEM((STEPS * TILE, ROWS), jnp.float32),
                pltpu.VMEM((STEPS * TILE, ROWS), jnp.float32),
                pltpu.VMEM((STEPS, 8, ROWS), jnp.float32),
                pltpu.VMEM((HEAD, ROWS), jnp.float32),
                pltpu.VMEM((ROWS, HEAD), jnp.bfloat16),
                pltpu.VMEM((ROWS, HEAD), jnp.bfloat16),
                pltpu.VMEM((TILE, 128), jnp.float32),
            ],
        ),
        out_shape=[jax.ShapeDtypeStruct((2 * HALF, WIDTH), jnp.bfloat16)] * 4
        + [jax.ShapeDtypeStruct((CHIPS, 4 * HALF, 2 * HEAD), jnp.bfloat16)],
        compiler_params=pltpu.CompilerParams(
            dimension_semantics=("arbitrary",), vmem_limit_bytes=36 * 2**20
        ),
        cost_estimate=pl.CostEstimate(flops=12 * 10**9, bytes_accessed=6 * 2**20, transcendentals=2 * 10**6),
        name="block_grads",
    )(core, table, lens, *own, *other, *pieces)


def gather(x):
    y = send(x, 0, 1)
    rx, lx = send(x, 1, 0), send(x, -1, 0)
    rxx = send(rx, 1, 0)
    ry, ly = send(y, 1, 0), send(y, -1, 0)
    lyy = send(ly, -1, 0)
    return x, y, rx, ry, lx, ly, rxx, lyy


def add(*xs):
    total = xs[0].astype(jnp.float32)
    for x in xs[1:]:
        total = total + x.astype(jnp.float32)
    return total


def scatter(w):
    low = lambda x: x.astype(jnp.bfloat16)
    a = send(w[6], -1, 0)
    b = send(w[7], 1, 0)
    d = send(w[4], 1, 0)
    e = send(w[3], -1, 0)
    f = send(low(add(w[2], a)), -1, 0)
    h = send(low(add(w[5], b)), 1, 0)
    i = send(low(add(w[1], e, h)), 0, 1)
    return add(w[0], d, f, i)


def local(query_one, query_two, keys, values, cotangent_one, cotangent_two, span_order, lengths):
    device = lax.axis_index("ctx")
    core = device % 2
    z, y = device // 2 // Y, device // 2 % Y
    half = HEADS_HERE * HEAD

    def mine(x, who, width):
        return lax.dynamic_slice(x, (0, who * width), (x.shape[0], width))

    def pairs(who):
        k, v = mine(keys, who, half), mine(values, who, half)
        return jnp.concatenate(
            [p[:, g * HEAD : (g + 1) * HEAD] for g in range(HEADS_HERE) for p in (k, v)], axis=1
        )

    here, there = pairs(core), send(pairs(1 - core), 0, 0, 1)
    xs = [
        jnp.concatenate([p[:, g * 2 * HEAD : (g + 1) * 2 * HEAD] for p in (here, there)], axis=0)
        for g in range(HEADS_HERE)
    ]
    slots = []
    for dz, dy in OFFSETS:
        chip = (z + dz + Z) % Z * Y + (y + dy) % Y
        slots += [4 * chip + 2 * core, 4 * chip + 2 * core + 1]
        slots += [4 * chip + 2 * (1 - core), 4 * chip + 2 * (1 - core) + 1]
    table = jnp.take(span_order, jnp.stack(slots))
    core_of = jnp.reshape(core, (1,))
    own = (query_one, query_two, cotangent_one, cotangent_two)
    other = [send(mine(x, 1 - core, HEADS_HERE * WIDTH), 0, 0, 1) for x in own]
    kept, got, sums = [[], []], [[], []], []
    for g in range(HEADS_HERE):
        pieces = gather(xs[g])
        *dqs, total = head_grads(g, core_of, table, lengths, own, other, pieces)
        for layer in range(2):
            kept[layer].append(dqs[layer])
            got[layer].append(send(dqs[2 + layer], 0, 0, 1))
        sums.append(scatter(total).astype(jnp.bfloat16))
    sums = jnp.stack(sums, axis=1)
    rows = 2 * HALF
    kv_kept, kv_got = sums[:rows], send(sums[rows:], 0, 0, 1)

    def whole(a, b):
        return jnp.where(core == 0, jnp.concatenate(a + b, axis=1), jnp.concatenate(b + a, axis=1))

    def heads(x, k):
        return [x[:, g, k * HEAD : (k + 1) * HEAD] for g in range(HEADS_HERE)]

    return (
        whole(kept[0], got[0]),
        whole(kept[1], got[1]),
        whole(heads(kv_kept, 0), heads(kv_got, 0)),
        whole(heads(kv_kept, 1), heads(kv_got, 1)),
    )


def solution(mesh):
    rows = P(("dp", "ctx"), None)
    return jax.shard_map(
        local,
        mesh=mesh,
        in_specs=(rows,) * 6 + (P("dp"), P("dp")),
        out_specs=(rows,) * 4,
        check_vma=False,
    )
```

time: 500 us -> 126 us (0.25); the launches traced: 490 us -> 124 us
  matrix products: 366 us -> 0 us
  starting transfers between devices: 0.11 us -> 50.3 us
  waiting for transfers between devices: 73 us -> 24.9 us
  Pallas kernels: 0 us -> 28.4 us
  other arithmetic: 20.2 us -> 5.18 us
  between operations: 14.3 us -> 0.98 us
    dot_general x32 -> x0, matrix products: 309 us -> none  [the longest x8 115 us: head_group(): jnp.einsum('htk,thd->kd', dscores_low, query_block, preferred_element_typ...]
    all_gather x2 -> x0, waiting for transfers between devices: 71.6 us -> none  [the longest x1 35.9 us: local(): lax.all_gather(common_values, 'ctx', axis=0, tiled=True)]
    sub x8 -> x0, matrix products: 56.5 us -> none  [head_group(): expo = jnp.exp(scores - peak)]
    ppermute x0 -> x38, starting transfers between devices: none -> 50.3 us  [send(): return lax.ppermute(x, 'ctx', moves(dz, dy, dcore))]
    pallas_call x0 -> x2, Pallas kernels: none -> 28.4 us  [head_grads(): pl.pallas_call(kernel, grid_spec=pltpu.PrefetchScalarGridSpec(num_scalar_...]
    ppermute x0 -> x38, waiting for transfers between devices: none -> 24.9 us  [send(): return lax.ppermute(x, 'ctx', moves(dz, dy, dcore))]
    add x2 -> x0, other arithmetic: 8.15 us -> none  [the longest x1 8.14 us: local(): stacked = jnp.concatenate([grad_k1 + grad_k2, grad_v1 + grad_v2], axis=1)]
    unnamed x74 -> x30, local copies, waits for them, and re-layouts: 12.7 us -> 5.28 us
  transfers between devices with their start and end apart: 3 -> 38, of which waited for: 2 -> 10; matrix products, arithmetic and copies ran while one was open for 29% -> 8% of each run, Pallas kernels for 0% -> 23%
where the time goes in v1:
time: 126 us; the launch traced here: 124 us
  starting transfers between devices  50.3 us (40%)
  Pallas kernels  28.4 us (23%)
  waiting for transfers between devices  24.9 us (20%)
  local copies, waits for them, and re-layouts  14.1 us (11%)
  other arithmetic  5.18 us (4%)
    ppermute x38, starting transfers between devices, send(): return lax.ppermute(x, 'ctx', moves(dz, dy, dcore))  50.3 us
    pallas_call x2, Pallas kernels, head_grads(): pl.pallas_call(kernel, grid_spec=pltpu.PrefetchScalarGridSpec(num_scalar_...  28.4 us
    ppermute x38, waiting for transfers between devices, send(): return lax.ppermute(x, 'ctx', moves(dz, dy, dcore))  24.9 us
    dynamic_slice x4, local copies, waits for them, and re-layouts, mine(): return lax.dynamic_slice(x, (0, who * width), (x.shape[0], width))  5.49 us
    unnamed x30, local copies, waits for them, and re-layouts  5.28 us
    select_n x4, other arithmetic, whole(): jnp.where(core == 0, jnp.concatenate(a + b, axis=1), jnp.concatenate(b +...  3.8 us
  transfers between devices with their start and end apart: 38, of which 10 were waited for; matrix products, arithmetic and copies ran while one was open for 8% of the time, Pallas kernels for 23%

profile of v1, /device:TPU:13, one launch (start us, length us, event | category | flops | bytes accessed | tf_op | source)
XLA Modules:
  0.0 123.8 jit_solution(6826417834474843419)
XLA Ops:
  3.1 1.9 %constant_dynamic-slice_fusion.11 = bf16[128,2048]{1,0:T(8,128)(2,1)} fusion(bf16[128,4096]{1,0:T(8,128)(2,1)} %refs_0_.3, s32[]{:T(128)S(6)} %select_n.138), kind=kLoop, calls=%fused_computation.61 | loop fusion | bytes 1048580 | tf_op jit(solution)/shard_map/dynamic_slice | solution.py:226
  6.4 2.1 %collective-permute-start.5 = (bf16[256,256]{1,0:T(8,128)(2,1)S(1)}, bf16[256,256]{1,0:T(8,128)(2,1)S(1)}, u32[]{:S(2)}, u32[]{:S(2)}) collective-permute-start(bf16[256,256]{1,0:T(8,128)(2,1)S(1)} %pad_maximum_fusion.2.refs_8_), channel_id=1, source_target_pairs={{0,2},{1,3},{2,0},{3,1},{4,6},{5,7},{6,4},{7,5},{8,10},{9,11},{10,... | collective-permute-start | bytes 393224 | tf_op jit(solution)/shard_map/ppermute | solution.py:47
  8.5 1.6 %collective-permute-start.6 = (bf16[256,256]{1,0:T(8,128)(2,1)S(1)}, bf16[256,256]{1,0:T(8,128)(2,1)}, u32[]{:S(2)}, u32[]{:S(2)}) collective-permute-start(bf16[256,256]{1,0:T(8,128)(2,1)S(1)} %pad_maximum_fusion.2.refs_8_), channel_id=1, source_target_pairs={{0,4},{1,5},{2,6},{3,7},{4,8},{5,9},{6,10},{7,11},{8,12},{9,13},{1... | collective-permute-start | bytes 393224 | tf_op jit(solution)/shard_map/ppermute | solution.py:47
  10.2 2.1 %collective-permute-start.8 = (bf16[256,256]{1,0:T(8,128)(2,1)S(1)}, bf16[256,256]{1,0:T(8,128)(2,1)}, u32[]{:S(2)}, u32[]{:S(2)}) collective-permute-start(bf16[256,256]{1,0:T(8,128)(2,1)S(1)} %pad_maximum_fusion.2.refs_8_), channel_id=1, source_target_pairs={{0,12},{1,13},{2,14},{3,15},{4,0},{5,1},{6,2},{7,3},{8,4},{9,5},{1... | collective-permute-start | bytes 393224 | tf_op jit(solution)/shard_map/ppermute | solution.py:47
  15.3 2.7 %collective-permute-start.9 = (bf16[256,256]{1,0:T(8,128)(2,1)S(1)}, bf16[256,256]{1,0:T(8,128)(2,1)S(1)}, u32[]{:S(2)}, u32[]{:S(2)}) collective-permute-start(bf16[256,256]{1,0:T(8,128)(2,1)S(1)} %collective-permute-done.5.refs_9_), channel_id=1, source_target_pairs={{0,12},{1,13},{2,14},{3,15},{4,0},{5,1},{6,2},{7,3},{8,4},{9,5},{1... | collective-permute-start | bytes 393224 | tf_op jit(solution)/shard_map/ppermute | solution.py:47
  18.1 1.9 %constant_dynamic-slice_fusion.8 = bf16[128,2048]{1,0:T(8,128)(2,1)} fusion(bf16[128,4096]{1,0:T(8,128)(2,1)} %refs_3_.3, s32[]{:T(128)S(6)} %select_n.138), kind=kLoop, calls=%fused_computation.58 | loop fusion | bytes 1048580 | tf_op jit(solution)/shard_map/dynamic_slice | solution.py:226
  22.6 3.2 %collective-permute-done.10.refs_14_ = bf16[256,256]{1,0:T(8,128)(2,1)S(1)} collective-permute-done((bf16[256,256]{1,0:T(8,128)(2,1)}, bf16[256,256]{1,0:T(8,128)(2,1)S(1)}, u32[]{:S(2)}, u32[]{:S(2)}) %collective-permute-start.10) | collective-permute-done | bytes 131104 | tf_op jit(solution)/shard_map/ppermute | solution.py:47
  26.5 2.2 %collective-permute-start.3 = (bf16[128,2048]{1,0:T(8,128)(2,1)}, bf16[128,2048]{1,0:T(8,128)(2,1)}, u32[]{:S(2)}, u32[]{:S(2)}) collective-permute-start(bf16[128,2048]{1,0:T(8,128)(2,1)} %constant_dynamic-slice_fusion.8), channel_id=1, source_target_pairs={{0,1},{1,0},{2,3},{3,2},{4,5},{5,4},{6,7},{7,6},{8,9},{9,8},{10,11... | collective-permute-start | bytes 1572872 | tf_op jit(solution)/shard_map/ppermute | solution.py:47
  30.5 4.3 %collective-permute-done.16.refs_13_ = bf16[256,256]{1,0:T(8,128)(2,1)} collective-permute-done((bf16[256,256]{1,0:T(8,128)(2,1)}, bf16[256,256]{1,0:T(8,128)(2,1)}, u32[]{:S(2)}, u32[]{:S(2)}) %collective-permute-start.16) | collective-permute-done | bytes 131104 | tf_op jit(solution)/shard_map/ppermute | solution.py:47
  36.3 2.9 %collective-permute-done.11.refs_15_ = bf16[256,256]{1,0:T(8,128)(2,1)S(1)} collective-permute-done((bf16[256,256]{1,0:T(8,128)(2,1)}, bf16[256,256]{1,0:T(8,128)(2,1)S(1)}, u32[]{:S(2)}, u32[]{:S(2)}) %collective-permute-start.11) | collective-permute-done | bytes 131104 | tf_op jit(solution)/shard_map/ppermute | solution.py:47
  39.2 2.7 %collective-permute-start.15 = (bf16[256,256]{1,0:T(8,128)(2,1)S(1)}, bf16[256,256]{1,0:T(8,128)(2,1)S(1)}, u32[]{:S(2)}, u32[]{:S(2)}) collective-permute-start(bf16[256,256]{1,0:T(8,128)(2,1)S(1)} %pad_maximum_fusion.3.refs_8_), channel_id=1, source_target_pairs={{0,12},{1,13},{2,14},{3,15},{4,0},{5,1},{6,2},{7,3},{8,4},{9,5},{1... | collective-permute-start | bytes 393224 | tf_op jit(solution)/shard_map/ppermute | solution.py:47
  42.1 2.7 %collective-permute-start.18 = (bf16[256,256]{1,0:T(8,128)(2,1)}, bf16[256,256]{1,0:T(8,128)(2,1)S(1)}, u32[]{:S(2)}, u32[]{:S(2)}) collective-permute-start(bf16[256,256]{1,0:T(8,128)(2,1)} %collective-permute-done.16.refs_13_), channel_id=1, source_target_pairs={{0,12},{1,13},{2,14},{3,15},{4,0},{5,1},{6,2},{7,3},{8,4},{9,5},{1... | collective-permute-start | bytes 393224 | tf_op jit(solution)/shard_map/ppermute | solution.py:47
  48.7 14.2 %block_grads.2 = (bf16[128,1024]{1,0:T(8,128)(2,1)S(1)}, bf16[128,1024]{1,0:T(8,128)(2,1)S(1)}, bf16[128,1024]{1,0:T(8,128)(2,1)S(1)}, bf16[128,1024]{1,0:T(8,128)(2,1)S(1)}, bf16[8,256,256]{2,1,0:T(8,128)(2,1)S(1)}) custom-call(s32[1]{0:T(128)} %bitcast.core, s32[32]{0:T(128)S(1)} %and_select_fusion.table, s32[8]{0:T(128)S(1)} %copy-done.14, ...), custom_call_target="tpu_custom_call" | custom-call | flops 12000000000 | bytes 6291456 | tf_op jit(solution)/shard_map/block_grads/pallas_call | solution.py:157
  65.8 14.2 %block_grads.3 = (bf16[128,1024]{1,0:T(8,128)(2,1)S(1)}, bf16[128,1024]{1,0:T(8,128)(2,1)S(1)}, bf16[128,1024]{1,0:T(8,128)(2,1)S(1)}, bf16[128,1024]{1,0:T(8,128)(2,1)S(1)}, bf16[8,256,256]{2,1,0:T(8,128)(2,1)S(1)}) custom-call(s32[1]{0:T(128)} %bitcast.core, s32[32]{0:T(128)S(1)} %and_select_fusion.table, s32[8]{0:T(128)S(1)} %copy-done.14, ...), custom_call_target="tpu_custom_call" | custom-call | flops 12000000000 | bytes 6291456 | tf_op jit(solution)/shard_map/block_grads/pallas_call | solution.py:157
  81.6 3.6 %collective-permute-start.21 = (bf16[128,1024]{1,0:T(8,128)(2,1)S(1)}, bf16[128,1024]{1,0:T(8,128)(2,1)S(1)}, u32[]{:S(2)}, u32[]{:S(2)}) collective-permute-start(bf16[128,1024]{1,0:T(8,128)(2,1)S(1)} %get-tuple-element.20), channel_id=1, source_target_pairs={{0,1},{1,0},{2,3},{3,2},{4,5},{5,4},{6,7},{7,6},{8,9},{9,8},{10,11... | collective-permute-start | bytes 786440 | tf_op jit(solution)/shard_map/ppermute | solution.py:47
  85.5 2.7 %collective-permute-start.33 = (bf16[256,256]{1,0:T(8,128)(2,1)S(1)}, bf16[256,256]{1,0:T(8,128)(2,1)S(1)}, u32[]{:S(2)}, u32[]{:S(2)}) collective-permute-start(bf16[256,256]{1,0:T(8,128)(2,1)S(1)} %get-tuple-element.32), channel_id=1, source_target_pairs={{0,12},{1,13},{2,14},{3,15},{4,0},{5,1},{6,2},{7,3},{8,4},{9,5},{1... | collective-permute-start | bytes 393224 | tf_op jit(solution)/shard_map/ppermute | solution.py:47
  88.2 3.3 %collective-permute-start.19 = (bf16[128,1024]{1,0:T(8,128)(2,1)S(1)}, bf16[128,1024]{1,0:T(8,128)(2,1)S(1)}, u32[]{:S(2)}, u32[]{:S(2)}) collective-permute-start(bf16[128,1024]{1,0:T(8,128)(2,1)S(1)} %get-tuple-element.16), channel_id=1, source_target_pairs={{0,1},{1,0},{2,3},{3,2},{4,5},{5,4},{6,7},{7,6},{8,9},{9,8},{10,11... | collective-permute-start | bytes 786440 | tf_op jit(solution)/shard_map/ppermute | solution.py:47
  97.0 4.6 %collective-permute-done.28 = bf16[256,256]{1,0:T(8,128)(2,1)S(1)} collective-permute-done((bf16[256,256]{1,0:T(8,128)(2,1)S(1)}, bf16[256,256]{1,0:T(8,128)(2,1)S(1)}, u32[]{:S(2)}, u32[]{:S(2)}) %collective-permute-start.28) | collective-permute-done | bytes 131104 | tf_op jit(solution)/shard_map/ppermute | solution.py:47
  101.7 2.7 %collective-permute-start.32 = (bf16[256,256]{1,0:T(8,128)(2,1)S(1)}, bf16[256,256]{1,0:T(8,128)(2,1)S(1)}, u32[]{:S(2)}, u32[]{:S(2)}) collective-permute-start(bf16[256,256]{1,0:T(8,128)(2,1)S(1)} %get-tuple-element.34), channel_id=1, source_target_pairs={{0,12},{1,13},{2,14},{3,15},{4,0},{5,1},{6,2},{7,3},{8,4},{9,5},{1... | collective-permute-start | bytes 393224 | tf_op jit(solution)/shard_map/ppermute | solution.py:47
  104.4 2.2 %collective-permute-done.35 = bf16[256,256]{1,0:T(8,128)(2,1)S(1)} collective-permute-done((bf16[256,256]{1,0:T(8,128)(2,1)S(1)}, bf16[256,256]{1,0:T(8,128)(2,1)S(1)}, u32[]{:S(2)}, u32[]{:S(2)}) %collective-permute-start.35) | collective-permute-done | bytes 131104 | tf_op jit(solution)/shard_map/ppermute | solution.py:47
  106.6 5.4 %collective-permute-start.29 = (bf16[256,256]{1,0:T(8,128)(2,1)S(1)}, bf16[256,256]{1,0:T(8,128)(2,1)S(1)}, u32[]{:S(2)}, u32[]{:S(2)}) collective-permute-start(bf16[256,256]{1,0:T(8,128)(2,1)S(1)} %fusion.9), channel_id=1, source_target_pairs={{0,2},{1,3},{2,0},{3,1},{4,6},{5,7},{6,4},{7,5},{8,10},{9,11},{10,... | collective-permute-start | bytes 393224 | tf_op jit(solution)/shard_map/ppermute | solution.py:47
  112.1 2.2 %collective-permute-done.29 = bf16[256,256]{1,0:T(8,128)(2,1)S(1)} collective-permute-done((bf16[256,256]{1,0:T(8,128)(2,1)S(1)}, bf16[256,256]{1,0:T(8,128)(2,1)S(1)}, u32[]{:S(2)}, u32[]{:S(2)}) %collective-permute-start.29) | collective-permute-done | bytes 131104 | tf_op jit(solution)/shard_map/ppermute | solution.py:47
  114.4 3.9 %collective-permute-done.36 = bf16[256,256]{1,0:T(8,128)(2,1)S(1)} collective-permute-done((bf16[256,256]{1,0:T(8,128)(2,1)S(1)}, bf16[256,256]{1,0:T(8,128)(2,1)S(1)}, u32[]{:S(2)}, u32[]{:S(2)}) %collective-permute-start.36) | collective-permute-done | bytes 131104 | tf_op jit(solution)/shard_map/ppermute | solution.py:47
  118.4 3.0 %collective-permute-start.37 = (bf16[128,2,256]{2,0,1:T(8,128)(2,1)S(1)}, bf16[128,2,256]{2,0,1:T(8,128)(2,1)S(1)}, u32[]{:S(2)}, u32[]{:S(2)}) collective-permute-start(bf16[128,2,256]{2,0,1:T(8,128)(2,1)S(1)} %pad_maximum_fusion), channel_id=1, source_target_pairs={{0,1},{1,0},{2,3},{3,2},{4,5},{5,4},{6,7},{7,6},{8,9},{9,8},{10,11... | collective-permute-start | bytes 393224 | tf_op jit(solution)/shard_map/ppermute | solution.py:47
  (115 shorter events, 30.5 us)
Async XLA Ops:
  6.4 8.9 %collective-permute-start.5 = (bf16[256,256]{1,0:T(8,128)(2,1)S(1)}, bf16[256,256]{1,0:T(8,128)(2,1)S(1)}, u32[]{:S(2)}, u32[]{:S(2)}) collective-permute-start(bf16[256,256]{1,0:T(8,128)(2,1)S(1)} %pad_maximum_fusion.2.refs_8_), channel_id=1, source_target_pairs={{0,2},{1,3},{2,0},{3,1},{4,6},{5,7},{6,4},{7,5},{8,10},{9,11},{10,... | collective-permute-start | bytes 393224 | tf_op jit(solution)/shard_map/ppermute | solution.py:47
  8.5 9.4 %collective-permute-start.6 = (bf16[256,256]{1,0:T(8,128)(2,1)S(1)}, bf16[256,256]{1,0:T(8,128)(2,1)}, u32[]{:S(2)}, u32[]{:S(2)}) collective-permute-start(bf16[256,256]{1,0:T(8,128)(2,1)S(1)} %pad_maximum_fusion.2.refs_8_), channel_id=1, source_target_pairs={{0,4},{1,5},{2,6},{3,7},{4,8},{5,9},{6,10},{7,11},{8,12},{9,13},{1... | collective-permute-start | bytes 393224 | tf_op jit(solution)/shard_map/ppermute | solution.py:47
  10.2 7.8 %collective-permute-start.8 = (bf16[256,256]{1,0:T(8,128)(2,1)S(1)}, bf16[256,256]{1,0:T(8,128)(2,1)}, u32[]{:S(2)}, u32[]{:S(2)}) collective-permute-start(bf16[256,256]{1,0:T(8,128)(2,1)S(1)} %pad_maximum_fusion.2.refs_8_), channel_id=1, source_target_pairs={{0,12},{1,13},{2,14},{3,15},{4,0},{5,1},{6,2},{7,3},{8,4},{9,5},{1... | collective-permute-start | bytes 393224 | tf_op jit(solution)/shard_map/ppermute | solution.py:47
  15.3 7.2 %collective-permute-start.9 = (bf16[256,256]{1,0:T(8,128)(2,1)S(1)}, bf16[256,256]{1,0:T(8,128)(2,1)S(1)}, u32[]{:S(2)}, u32[]{:S(2)}) collective-permute-start(bf16[256,256]{1,0:T(8,128)(2,1)S(1)} %collective-permute-done.5.refs_9_), channel_id=1, source_target_pairs={{0,12},{1,13},{2,14},{3,15},{4,0},{5,1},{6,2},{7,3},{8,4},{9,5},{1... | collective-permute-start | bytes 393224 | tf_op jit(solution)/shard_map/ppermute | solution.py:47
  18.0 10.7 %collective-permute-start.7 = (bf16[256,256]{1,0:T(8,128)(2,1)S(1)}, bf16[256,256]{1,0:T(8,128)(2,1)S(1)}, u32[]{:S(2)}, u32[]{:S(2)}) collective-permute-start(bf16[256,256]{1,0:T(8,128)(2,1)S(1)} %collective-permute-done.5.refs_9_), channel_id=1, source_target_pairs={{0,4},{1,5},{2,6},{3,7},{4,8},{5,9},{6,10},{7,11},{8,12},{9,13},{1... | collective-permute-start | bytes 393224 | tf_op jit(solution)/shard_map/ppermute | solution.py:47
  18.0 7.8 %collective-permute-start.10 = (bf16[256,256]{1,0:T(8,128)(2,1)}, bf16[256,256]{1,0:T(8,128)(2,1)S(1)}, u32[]{:S(2)}, u32[]{:S(2)}) collective-permute-start(bf16[256,256]{1,0:T(8,128)(2,1)} %collective-permute-done.6.refs_10_), channel_id=1, source_target_pairs={{0,4},{1,5},{2,6},{3,7},{4,8},{5,9},{6,10},{7,11},{8,12},{9,13},{1... | collective-permute-start | bytes 393224 | tf_op jit(solution)/shard_map/ppermute | solution.py:47
  20.4 21.6 %collective-permute-start = (bf16[128,2048]{1,0:T(8,128)(2,1)}, bf16[128,2048]{1,0:T(8,128)(2,1)}, u32[]{:S(2)}, u32[]{:S(2)}) collective-permute-start(bf16[128,2048]{1,0:T(8,128)(2,1)} %constant_dynamic-slice_fusion.11), channel_id=1, source_target_pairs={{0,1},{1,0},{2,3},{3,2},{4,5},{5,4},{6,7},{7,6},{8,9},{9,8},{10,11... | collective-permute-start | bytes 1572872 | tf_op jit(solution)/shard_map/ppermute | solution.py:47
  21.9 20.1 %collective-permute-start.1 = (bf16[128,2048]{1,0:T(8,128)(2,1)}, bf16[128,2048]{1,0:T(8,128)(2,1)}, u32[]{:S(2)}, u32[]{:S(2)}) collective-permute-start(bf16[128,2048]{1,0:T(8,128)(2,1)} %constant_dynamic-slice_fusion.10), channel_id=1, source_target_pairs={{0,1},{1,0},{2,3},{3,2},{4,5},{5,4},{6,7},{7,6},{8,9},{9,8},{10,11... | collective-permute-start | bytes 1572872 | tf_op jit(solution)/shard_map/ppermute | solution.py:47
  22.5 19.6 %collective-permute-start.2 = (bf16[128,2048]{1,0:T(8,128)(2,1)}, bf16[128,2048]{1,0:T(8,128)(2,1)}, u32[]{:S(2)}, u32[]{:S(2)}) collective-permute-start(bf16[128,2048]{1,0:T(8,128)(2,1)} %constant_dynamic-slice_fusion.9), channel_id=1, source_target_pairs={{0,1},{1,0},{2,3},{3,2},{4,5},{5,4},{6,7},{7,6},{8,9},{9,8},{10,11... | collective-permute-start | bytes 1572872 | tf_op jit(solution)/shard_map/ppermute | solution.py:47
  26.5 18.3 %collective-permute-start.3 = (bf16[128,2048]{1,0:T(8,128)(2,1)}, bf16[128,2048]{1,0:T(8,128)(2,1)}, u32[]{:S(2)}, u32[]{:S(2)}) collective-permute-start(bf16[128,2048]{1,0:T(8,128)(2,1)} %constant_dynamic-slice_fusion.8), channel_id=1, source_target_pairs={{0,1},{1,0},{2,3},{3,2},{4,5},{5,4},{6,7},{7,6},{8,9},{9,8},{10,11... | collective-permute-start | bytes 1572872 | tf_op jit(solution)/shard_map/ppermute | solution.py:47
  39.2 23.8 %collective-permute-start.15 = (bf16[256,256]{1,0:T(8,128)(2,1)S(1)}, bf16[256,256]{1,0:T(8,128)(2,1)S(1)}, u32[]{:S(2)}, u32[]{:S(2)}) collective-permute-start(bf16[256,256]{1,0:T(8,128)(2,1)S(1)} %pad_maximum_fusion.3.refs_8_), channel_id=1, source_target_pairs={{0,12},{1,13},{2,14},{3,15},{4,0},{5,1},{6,2},{7,3},{8,4},{9,5},{1... | collective-permute-start | bytes 393224 | tf_op jit(solution)/shard_map/ppermute | solution.py:47
  42.0 22.5 %collective-permute-start.14 = (bf16[256,256]{1,0:T(8,128)(2,1)}, bf16[256,256]{1,0:T(8,128)(2,1)S(1)}, u32[]{:S(2)}, u32[]{:S(2)}) collective-permute-start(bf16[256,256]{1,0:T(8,128)(2,1)} %collective-permute-done.12.refs_9_), channel_id=1, source_target_pairs={{0,4},{1,5},{2,6},{3,7},{4,8},{5,9},{6,10},{7,11},{8,12},{9,13},{1... | collective-permute-start | bytes 393224 | tf_op jit(solution)/shard_map/ppermute | solution.py:47
  42.0 23.8 %collective-permute-start.17 = (bf16[256,256]{1,0:T(8,128)(2,1)}, bf16[256,256]{1,0:T(8,128)(2,1)S(1)}, u32[]{:S(2)}, u32[]{:S(2)}) collective-permute-start(bf16[256,256]{1,0:T(8,128)(2,1)} %copy-done.6), channel_id=1, source_target_pairs={{0,4},{1,5},{2,6},{3,7},{4,8},{5,9},{6,10},{7,11},{8,12},{9,13},{1... | collective-permute-start | bytes 393224 | tf_op jit(solution)/shard_map/ppermute | solution.py:47
  42.1 23.7 %collective-permute-start.18 = (bf16[256,256]{1,0:T(8,128)(2,1)}, bf16[256,256]{1,0:T(8,128)(2,1)S(1)}, u32[]{:S(2)}, u32[]{:S(2)}) collective-permute-start(bf16[256,256]{1,0:T(8,128)(2,1)} %collective-permute-done.16.refs_13_), channel_id=1, source_target_pairs={{0,12},{1,13},{2,14},{3,15},{4,0},{5,1},{6,2},{7,3},{8,4},{9,5},{1... | collective-permute-start | bytes 393224 | tf_op jit(solution)/shard_map/ppermute | solution.py:47
  62.9 18.7 %collective-permute-start.24 = (bf16[256,256]{1,0:T(8,128)(2,1)S(1)}, bf16[256,256]{1,0:T(8,128)(2,1)S(1)}, u32[]{:S(2)}, u32[]{:S(2)}) collective-permute-start(bf16[256,256]{1,0:T(8,128)(2,1)S(1)} %get-tuple-element.27), channel_id=1, source_target_pairs={{0,12},{1,13},{2,14},{3,15},{4,0},{5,1},{6,2},{7,3},{8,4},{9,5},{1... | collective-permute-start | bytes 393224 | tf_op jit(solution)/shard_map/ppermute | solution.py:47
  63.0 22.2 %collective-permute-start.27 = (bf16[256,256]{1,0:T(8,128)(2,1)S(1)}, bf16[256,256]{1,0:T(8,128)(2,1)S(1)}, u32[]{:S(2)}, u32[]{:S(2)}) collective-permute-start(bf16[256,256]{1,0:T(8,128)(2,1)S(1)} %get-tuple-element.25), channel_id=1, source_target_pairs={{0,4},{1,5},{2,6},{3,7},{4,8},{5,9},{6,10},{7,11},{8,12},{9,13},{1... | collective-permute-start | bytes 393224 | tf_op jit(solution)/shard_map/ppermute | solution.py:47
  64.5 31.2 %collective-permute-start.26 = (bf16[256,256]{1,0:T(8,128)(2,1)S(1)}, bf16[256,256]{1,0:T(8,128)(2,1)S(1)}, u32[]{:S(2)}, u32[]{:S(2)}) collective-permute-start(bf16[256,256]{1,0:T(8,128)(2,1)S(1)} %get-tuple-element.26), channel_id=1, source_target_pairs={{0,12},{1,13},{2,14},{3,15},{4,0},{5,1},{6,2},{7,3},{8,4},{9,5},{1... | collective-permute-start | bytes 393224 | tf_op jit(solution)/shard_map/ppermute | solution.py:47
  85.4 26.6 %collective-permute-start.23 = (bf16[256,256]{1,0:T(8,128)(2,1)S(1)}, bf16[256,256]{1,0:T(8,128)(2,1)S(1)}, u32[]{:S(2)}, u32[]{:S(2)}) collective-permute-start(bf16[256,256]{1,0:T(8,128)(2,1)S(1)} %get-tuple-element.24), channel_id=1, source_target_pairs={{0,4},{1,5},{2,6},{3,7},{4,8},{5,9},{6,10},{7,11},{8,12},{9,13},{1... | collective-permute-start | bytes 393224 | tf_op jit(solution)/shard_map/ppermute | solution.py:47
  85.5 16.1 %collective-permute-start.33 = (bf16[256,256]{1,0:T(8,128)(2,1)S(1)}, bf16[256,256]{1,0:T(8,128)(2,1)S(1)}, u32[]{:S(2)}, u32[]{:S(2)}) collective-permute-start(bf16[256,256]{1,0:T(8,128)(2,1)S(1)} %get-tuple-element.32), channel_id=1, source_target_pairs={{0,12},{1,13},{2,14},{3,15},{4,0},{5,1},{6,2},{7,3},{8,4},{9,5},{1... | collective-permute-start | bytes 393224 | tf_op jit(solution)/shard_map/ppermute | solution.py:47
  92.9 21.5 %collective-permute-start.30 = (bf16[256,256]{1,0:T(8,128)(2,1)S(1)}, bf16[256,256]{1,0:T(8,128)(2,1)S(1)}, u32[]{:S(2)}, u32[]{:S(2)}) collective-permute-start(bf16[256,256]{1,0:T(8,128)(2,1)S(1)} %get-tuple-element.30), channel_id=1, source_target_pairs={{0,4},{1,5},{2,6},{3,7},{4,8},{5,9},{6,10},{7,11},{8,12},{9,13},{1... | collective-permute-start | bytes 393224 | tf_op jit(solution)/shard_map/ppermute | solution.py:47
  93.1 8.5 %collective-permute-start.28 = (bf16[256,256]{1,0:T(8,128)(2,1)S(1)}, bf16[256,256]{1,0:T(8,128)(2,1)S(1)}, u32[]{:S(2)}, u32[]{:S(2)}) collective-permute-start(bf16[256,256]{1,0:T(8,128)(2,1)S(1)} %get-tuple-element.29), channel_id=1, source_target_pairs={{0,4},{1,5},{2,6},{3,7},{4,8},{5,9},{6,10},{7,11},{8,12},{9,13},{1... | collective-permute-start | bytes 393224 | tf_op jit(solution)/shard_map/ppermute | solution.py:47
  95.7 16.4 %collective-permute-start.25 = (bf16[256,256]{1,0:T(8,128)(2,1)S(1)}, bf16[256,256]{1,0:T(8,128)(2,1)S(1)}, u32[]{:S(2)}, u32[]{:S(2)}) collective-permute-start(bf16[256,256]{1,0:T(8,128)(2,1)S(1)} %get-tuple-element.28), channel_id=1, source_target_pairs={{0,12},{1,13},{2,14},{3,15},{4,0},{5,1},{6,2},{7,3},{8,4},{9,5},{1... | collective-permute-start | bytes 393224 | tf_op jit(solution)/shard_map/ppermute | solution.py:47
  101.7 12.8 %collective-permute-start.32 = (bf16[256,256]{1,0:T(8,128)(2,1)S(1)}, bf16[256,256]{1,0:T(8,128)(2,1)S(1)}, u32[]{:S(2)}, u32[]{:S(2)}) collective-permute-start(bf16[256,256]{1,0:T(8,128)(2,1)S(1)} %get-tuple-element.34), channel_id=1, source_target_pairs={{0,12},{1,13},{2,14},{3,15},{4,0},{5,1},{6,2},{7,3},{8,4},{9,5},{1... | collective-permute-start | bytes 393224 | tf_op jit(solution)/shard_map/ppermute | solution.py:47
  106.6 7.7 %collective-permute-start.29 = (bf16[256,256]{1,0:T(8,128)(2,1)S(1)}, bf16[256,256]{1,0:T(8,128)(2,1)S(1)}, u32[]{:S(2)}, u32[]{:S(2)}) collective-permute-start(bf16[256,256]{1,0:T(8,128)(2,1)S(1)} %fusion.9), channel_id=1, source_target_pairs={{0,2},{1,3},{2,0},{3,1},{4,6},{5,7},{6,4},{7,5},{8,10},{9,11},{10,... | collective-permute-start | bytes 393224 | tf_op jit(solution)/shard_map/ppermute | solution.py:47
  (29 other events, 214.4 us)

commit v2 on v1

v2 whole, which is shorter than its diff:
```python
import math

import jax
import jax.numpy as jnp
from jax import lax
from jax.experimental import pallas as pl
from jax.experimental.pallas import tpu as pltpu
from jax.sharding import PartitionSpec as P

HEAD = 128
KEY_VALUE_HEADS = 4
QUERY_PER_KEY = 8
HALF = 64
MOST = 1024
NEG = -1e30
SCALE = HEAD**-0.5
LOG2E = math.log2(math.e)
Z, Y = 4, 2
CHIPS = Z * Y
TOKENS = 2048
BLOCKS = TOKENS // HALF
SHARE = KEY_VALUE_HEADS // 2
HEADS = 1
PART = HEADS * HEAD
WIDTH = QUERY_PER_KEY * HEAD
ROWS = 2 * QUERY_PER_KEY * HALF
TILE = 512
TAILS = (128, 256, 384)
PAD = TILE
KEYS = (MOST + HALF + TAILS[0]) // TAILS[0] * TAILS[0]
LANES = 512
CHUNKS = [(g, c) for g in range(HEADS) for c in range(ROWS // LANES)]


def device_of(z, y, core):
    return ((z % Z) * Y + y % Y) * 2 + core


def swap(x):
    return lax.ppermute(x, "ctx", [(d, d ^ 1) for d in range(CHIPS * 2)])


def exchange(x):
    groups = [[device_of(z, y, c) for z in range(Z) for y in range(Y)] for c in range(2)]
    return lax.all_to_all(x, "ctx", 0, 0, axis_index_groups=groups, tiled=True)


def block_grads(position, lens, qs, gs, dqs, ks, vs, dk, dv, es, dps, ms, dqt, qst, gst, bias):
    token = lax.broadcasted_iota(jnp.int32, (1, 128), 1) % HALF
    where = position * HALF + token
    starts = jnp.zeros((1, 128), jnp.int32)
    low = jnp.int32(0)
    end = jnp.int32(0)
    for k in range(lens.shape[0]):
        end = end + lens[k]
        starts = jnp.where(where >= end, end, starts)
        low = jnp.where(position * HALF >= end, end, low)
    stop = (position + 1) * HALF
    count = stop - low
    steps = (count + TILE - TAILS[-1] - 1) // TILE
    rest = count - steps * TILE
    short = [(low < rest) & (rest <= size) for low, size in zip((0, *TAILS), TAILS)]
    for g in range(HEADS):
        for layer in range(2):
            for h in range(QUERY_PER_KEY):
                r = (layer * QUERY_PER_KEY + h) * HALF
                col = (g * QUERY_PER_KEY + h) * HEAD
                qst[g, r : r + HALF, :] = qs[layer][:, col : col + HEAD]
                gst[g, r : r + HALF, :] = gs[layer][:, col : col + HEAD]
    by_head = (((1,), (1,)), ((), ()))

    def scores(t, at, size, carry):
        base = stop - at - size
        row = pl.multiple_of(base + PAD, HALF)
        key = base + lax.broadcasted_iota(jnp.int32, (size, 128), 0)
        bias[:size, :] = jnp.where((key <= where) & (key >= starts), 0.0, NEG)
        out = []
        for i, (g, c) in enumerate(CHUNKS):
            top, total, mean = carry[i]
            sl = slice(c * LANES, (c + 1) * LANES)
            to = slice(i * LANES, (i + 1) * LANES)
            kt = ks[g, pl.ds(row, size), :]
            vt = vs[g, pl.ds(row, size), :]
            s = lax.dot_general(kt, qst[g, sl, :], by_head, preferred_element_type=jnp.float32)
            dp = lax.dot_general(vt, gst[g, sl, :], by_head, preferred_element_type=jnp.float32)
            s = s * (SCALE * LOG2E) + jnp.concatenate([bias[:size, :]] * (LANES // 128), axis=1)
            now = jnp.maximum(top, jnp.max(s, axis=0, keepdims=True))
            e = jnp.exp2(s - now)
            shrink = jnp.exp2(top - now)
            total = total * shrink + jnp.sum(e, axis=0, keepdims=True)
            mean = mean * shrink + jnp.sum(e * dp, axis=0, keepdims=True)
            es[pl.ds(at, size), to] = e
            dps[pl.ds(at, size), to] = dp
            ms[t, :, to] = jnp.broadcast_to(now, (8, LANES))
            out.append((now, total, mean))
        return tuple(out)

    zero = jnp.zeros((1, LANES), jnp.float32)
    found = tuple((zero + NEG, zero, zero) for _ in CHUNKS)
    at_rest = pl.multiple_of(steps * TILE, TILE)
    found = lax.fori_loop(0, steps, lambda t, f: scores(t, pl.multiple_of(t * TILE, TILE), TILE, f), found)
    for taken, size in zip(short, TAILS):
        found = lax.cond(taken, lambda f, size=size: scores(steps, at_rest, size, f), lambda f: f, found)
    inverse = [1.0 / f[1] for f in found]
    dsum = [f[2] * i for f, i in zip(found, inverse)]
    dqt[...] = jnp.zeros_like(dqt)

    def grads(t, at, size):
        row = pl.multiple_of(stop - at - size + PAD, HALF)
        for i, (g, c) in enumerate(CHUNKS):
            sl = slice(c * LANES, (c + 1) * LANES)
            to = slice(i * LANES, (i + 1) * LANES)
            kt = ks[g, pl.ds(row, size), :]
            p = es[pl.ds(at, size), to] * (jnp.exp2(ms[t, 0:1, to] - found[i][0]) * inverse[i])
            ds = (p * (dps[pl.ds(at, size), to] - dsum[i]) * SCALE).astype(jnp.bfloat16)
            dv[g, pl.ds(row, size), :] += jnp.dot(
                p.astype(jnp.bfloat16), gst[g, sl, :], preferred_element_type=jnp.float32
            )
            dk[g, pl.ds(row, size), :] += jnp.dot(ds, qst[g, sl, :], preferred_element_type=jnp.float32)
            dqt[:, to] += lax.dot_general(kt, ds, (((0,), (0,)), ((), ())), preferred_element_type=jnp.float32)

    lax.fori_loop(0, steps, lambda t, _: grads(t, pl.multiple_of(t * TILE, TILE), TILE), None)

    for taken, size in zip(short, TAILS):
        pl.when(taken)(lambda size=size: grads(steps, at_rest, size))

    for g in range(HEADS):
        for layer in range(2):
            for h in range(0, QUERY_PER_KEY, 2):
                r = g * ROWS + (layer * QUERY_PER_KEY + h) * HALF
                col = (g * QUERY_PER_KEY + h) * HEAD
                x = dqt[:, r : r + 128].astype(jnp.bfloat16).T
                dqs[layer][:, col : col + HEAD] = x[:HALF]
                dqs[layer][:, col + HEAD : col + 2 * HEAD] = x[HALF:]


def kernel(place, spans, lens, *refs):
    own, other, gathered, outs, total, scratch = refs[:4], refs[4:8], refs[8], refs[9:13], refs[13], refs[14:]
    ks, vs, dk, dv = scratch[:4]
    step = pl.program_id(0)
    core, chip = place[0] & 1, place[0] >> 1

    def position(k, s):
        return spans[4 * k + 2 * (core if s < 2 else 1 - core) + s % 2]

    @pl.when(step == 0)
    def _():
        ks[:, :PAD, :] = jnp.zeros((HEADS, PAD, HEAD), jnp.bfloat16)
        vs[:, :PAD, :] = jnp.zeros((HEADS, PAD, HEAD), jnp.bfloat16)
        dk[...] = jnp.zeros_like(dk)
        dv[...] = jnp.zeros_like(dv)
        for k in range(CHIPS):
            for s in range(4):
                p = pl.multiple_of(position(k, s) * HALF + PAD, HALF)
                x = gathered[k, s * HALF : (s + 1) * HALF, :]
                for g in range(HEADS):
                    ks[g, pl.ds(p, HALF), :] = x[:, g * HEAD : (g + 1) * HEAD]
                    vs[g, pl.ds(p, HALF), :] = x[:, PART + g * HEAD : PART + (g + 1) * HEAD]

    first = spans[4 * chip + 2 * core + step]
    second = spans[4 * chip + 2 * (1 - core) + step]
    block_grads(first, lens, own[:2], own[2:], outs[:2], *scratch)
    block_grads(second, lens, other[:2], other[2:], outs[2:], *scratch)

    @pl.when(step == 1)
    def _():
        for k in range(CHIPS):
            for s in range(4):
                p = pl.multiple_of(position(k, s) * HALF + PAD, HALF)
                rows = slice(s * HALF, (s + 1) * HALF)
                for g in range(HEADS):
                    cols = slice(g * HEAD, (g + 1) * HEAD)
                    total[k, rows, cols] = dk[g, pl.ds(p, HALF), :].astype(jnp.bfloat16)
                    cols = slice(PART + g * HEAD, PART + (g + 1) * HEAD)
                    total[k, rows, cols] = dv[g, pl.ds(p, HALF), :].astype(jnp.bfloat16)


def chip_grads(g, place, spans, lens, own, other, gathered):
    by_core = pl.BlockSpec((HALF, HEADS * WIDTH), lambda s, place, *_: (s, (place[0] & 1) * SHARE + g))
    by_step = pl.BlockSpec((HALF, HEADS * WIDTH), lambda s, *_: (s, 0))
    all_chips = pl.BlockSpec((CHIPS, 4 * HALF, 2 * PART), lambda s, *_: (0, 0, 0))
    return pl.pallas_call(
        kernel,
        grid_spec=pltpu.PrefetchScalarGridSpec(
            num_scalar_prefetch=3,
            grid=(2,),
            in_specs=[by_core] * 8 + [all_chips],
            out_specs=[by_step] * 4 + [all_chips],
            scratch_shapes=[
                pltpu.VMEM((HEADS, TOKENS + PAD, HEAD), jnp.bfloat16),
                pltpu.VMEM((HEADS, TOKENS + PAD, HEAD), jnp.bfloat16),
                pltpu.VMEM((HEADS, TOKENS + PAD, HEAD), jnp.float32),
                pltpu.VMEM((HEADS, TOKENS + PAD, HEAD), jnp.float32),
                pltpu.VMEM((KEYS, HEADS * ROWS), jnp.float32),
                pltpu.VMEM((KEYS, HEADS * ROWS), jnp.float32),
                pltpu.VMEM((KEYS // TILE + 1, 8, HEADS * ROWS), jnp.float32),
                pltpu.VMEM((HEAD, HEADS * ROWS), jnp.float32),
                pltpu.VMEM((HEADS, ROWS, HEAD), jnp.bfloat16),
                pltpu.VMEM((HEADS, ROWS, HEAD), jnp.bfloat16),
                pltpu.VMEM((TILE, 128), jnp.float32),
            ],
        ),
        out_shape=[jax.ShapeDtypeStruct((2 * HALF, HEADS * WIDTH), jnp.bfloat16)] * 4
        + [jax.ShapeDtypeStruct((CHIPS, 4 * HALF, 2 * PART), jnp.bfloat16)],
        compiler_params=pltpu.CompilerParams(
            dimension_semantics=("arbitrary",), vmem_limit_bytes=60 * 2**20
        ),
        cost_estimate=pl.CostEstimate(flops=12 * 10**9, bytes_accessed=6 * 2**20, transcendentals=2 * 10**6),
        name="chip_grads",
    )(place, spans, lens, *own, *other, gathered)


def local(query_one, query_two, keys, values, cotangent_one, cotangent_two, span_order, lengths):
    device = lax.axis_index("ctx")
    core = device & 1

    def parts(who):
        k, v = [lax.dynamic_slice(x, (0, who * SHARE * HEAD), (2 * HALF, SHARE * HEAD)) for x in (keys, values)]
        return [x[:, g * HEAD : (g + 1) * HEAD] for g in range(SHARE) for x in (k, v)]

    theirs = swap(jnp.concatenate(parts(1 - core), axis=1))
    mine = parts(core)
    sent = []
    for g in range(SHARE):
        x = jnp.concatenate(mine[2 * g : 2 * g + 2], axis=1)
        x = jnp.concatenate([x, theirs[:, 2 * g * HEAD : (2 * g + 2) * HEAD]], axis=0)
        sent.append(jnp.broadcast_to(x, (CHIPS, *x.shape)))
    own = (query_one, query_two, cotangent_one, cotangent_two)
    own, sent[0] = lax.optimization_barrier((own, sent[0]))
    other = [swap(a) for a in own]
    place = jnp.reshape(device, (1,))
    grads, sums = [], []
    for g in range(SHARE):
        *dqs, total = chip_grads(g, place, span_order, lengths, own, other, exchange(sent[g]))
        grads.append(dqs)
        sums.append(jnp.sum(exchange(total).astype(jnp.float32), axis=0).astype(jnp.bfloat16))
    got = swap(jnp.concatenate([x[2 * HALF :] for x in sums], axis=1))
    kept = jnp.concatenate([x[: 2 * HALF] for x in sums], axis=1)

    def whole(a, b):
        return jnp.where(core == 0, jnp.concatenate(a + b, axis=1), jnp.concatenate(b + a, axis=1))

    def heads(x, k):
        return [x[:, (2 * g + k) * HEAD : (2 * g + k + 1) * HEAD] for g in range(SHARE)]

    return (
        whole([d[0] for d in grads], [swap(d[2]) for d in grads]),
        whole([d[1] for d in grads], [swap(d[3]) for d in grads]),
        whole(heads(kept, 0), heads(got, 0)),
        whole(heads(kept, 1), heads(got, 1)),
    )


def solution(mesh):
    rows = P(("dp", "ctx"), None)
    return jax.shard_map(
        local,
        mesh=mesh,
        in_specs=(rows,) * 6 + (P("dp"), P("dp")),
        out_specs=(rows,) * 4,
        check_vma=False,
    )
```

time: 126 us -> 105 us (0.83)
  starting transfers between devices: 50.3 us -> 31.6 us
  waiting for transfers between devices: 24.9 us -> 40.3 us
  local copies, waits for them, and re-layouts: 14.1 us -> 4.31 us
  Pallas kernels: 28.4 us -> 21.3 us
    ppermute x38 -> x10, starting transfers between devices: 50.3 us -> 5.59 us  [swap(): return lax.ppermute(x, 'ctx', [(d, d ^ 1) for d in range(CHIPS * 2)])]
    all_to_all x0 -> x4, waiting for transfers between devices: none -> 38.3 us  [exchange(): return lax.all_to_all(x, 'ctx', 0, 0, axis_index_groups=groups, tiled=True)]
    all_to_all x0 -> x4, starting transfers between devices: none -> 26 us  [exchange(): return lax.all_to_all(x, 'ctx', 0, 0, axis_index_groups=groups, tiled=True)]
    ppermute x38 -> x10, waiting for transfers between devices: 24.9 us -> 1.99 us  [swap(): return lax.ppermute(x, 'ctx', [(d, d ^ 1) for d in range(CHIPS * 2)])]
    pallas_call x2, Pallas kernels: 28.4 us -> 21.3 us  [chip_grads(): pl.pallas_call(kernel, grid_spec=pltpu.PrefetchScalarGridSpec(num_scalar_...]
    dynamic_slice x4 -> x0, local copies, waits for them, and re-layouts: 5.49 us -> none  [mine(): return lax.dynamic_slice(x, (0, who * width), (x.shape[0], width))]
    unnamed x30 -> x14, local copies, waits for them, and re-layouts: 5.28 us -> 1.21 us
    broadcast_in_dim x0 -> x2, local copies, waits for them, and re-layouts: none -> 2.14 us  [local(): sent.append(jnp.broadcast_to(x, (CHIPS, *x.shape)))]
  transfers between devices with their start and end apart: 38 -> 14, of which waited for: 10 -> 6; matrix products, arithmetic and copies ran while one was open for 8% -> 5% of each run, Pallas kernels for 23% -> 21%
where the time goes in v2:
time: 105 us; the launch traced here: 104 us
  waiting for transfers between devices  40.3 us (38%)
  starting transfers between devices  31.6 us (30%)
  Pallas kernels  21.3 us (20%)
  other arithmetic  5.26 us (5%)
  local copies, waits for them, and re-layouts  4.31 us (4%)
    all_to_all x4, waiting for transfers between devices, exchange(): return lax.all_to_all(x, 'ctx', 0, 0, axis_index_groups=groups, tiled=True)  38.3 us
    all_to_all x4, starting transfers between devices, exchange(): return lax.all_to_all(x, 'ctx', 0, 0, axis_index_groups=groups, tiled=True)  26 us
    pallas_call x2, Pallas kernels, chip_grads(): pl.pallas_call(kernel, grid_spec=pltpu.PrefetchScalarGridSpec(num_scalar_...  21.3 us
    ppermute x10, starting transfers between devices, swap(): return lax.ppermute(x, 'ctx', [(d, d ^ 1) for d in range(CHIPS * 2)])  5.59 us
    select_n x4, other arithmetic, whole(): jnp.where(core == 0, jnp.concatenate(a + b, axis=1), jnp.concatenate(b +...  4.91 us
    broadcast_in_dim x2, local copies, waits for them, and re-layouts, local(): sent.append(jnp.broadcast_to(x, (CHIPS, *x.shape)))  2.14 us
  transfers between devices with their start and end apart: 14, of which 6 were waited for; matrix products, arithmetic and copies ran while one was open for 5% of the time, Pallas kernels for 21%

profile of v2, /device:TPU:13, one launch (start us, length us, event | category | flops | bytes accessed | tf_op | source)
XLA Modules:
  0.0 103.6 jit_solution(5120780322315954577)
XLA Ops:
  0.6 0.9 constant_dynamic-slice_fusion.6
  1.6 0.8 collective-permute-start
  2.3 1.0 collective-permute-done
  3.4 1.0 %broadcast_in_dim.6 = bf16[8,256,256]{2,1,0:T(8,128)(2,1)} broadcast(bf16[256,256]{1,0:T(8,128)(2,1)S(1)} %pad_maximum_fusion.1), dimensions={1,2} | broadcast | bytes 1179648 | tf_op jit(solution)/shard_map/broadcast_in_dim | solution.py:227
  4.4 0.4 collective-permute-start.1
  5.4 6.8 %all-to-all-start = ((bf16[8,256,256]{2,1,0:T(8,128)(2,1)}), bf16[8,256,256]{2,1,0:T(8,128)(2,1)S(1)}, u32[]{:S(2)}, u32[]{:S(2)}) async-start(bf16[8,256,256]{2,1,0:T(8,128)(2,1)} %broadcast_in_dim.6), calls=%async_computation | async-start | bytes 2097152 | tf_op jit(solution)/shard_map/all_to_all | solution.py:45
  12.2 16.6 %all-to-all-done.refs_8_ = bf16[8,256,256]{2,1,0:T(8,128)(2,1)S(1)} async-done(((bf16[8,256,256]{2,1,0:T(8,128)(2,1)}), bf16[8,256,256]{2,1,0:T(8,128)(2,1)S(1)}, u32[]{:S(2)}, u32[]{:S(2)}) %all-to-all-start) | async-done | bytes 1048608 | tf_op jit(solution)/shard_map/all_to_all | solution.py:45
  28.8 1.1 %broadcast_in_dim.7 = bf16[8,256,256]{2,1,0:T(8,128)(2,1)} broadcast(bf16[256,256]{1,0:T(8,128)(2,1)S(1)} %pad_maximum_fusion.2), dimensions={1,2} | broadcast | bytes 1179648 | tf_op jit(solution)/shard_map/broadcast_in_dim | solution.py:227
  30.2 3.6 %all-to-all-start.1 = ((bf16[8,256,256]{2,1,0:T(8,128)(2,1)}), bf16[8,256,256]{2,1,0:T(8,128)(2,1)S(1)}, u32[]{:S(2)}, u32[]{:S(2)}) async-start(bf16[8,256,256]{2,1,0:T(8,128)(2,1)} %broadcast_in_dim.7), calls=%async_computation.1 | async-start | bytes 2097152 | tf_op jit(solution)/shard_map/all_to_all | solution.py:45
  33.8 10.6 %chip_grads.2 = (bf16[128,1024]{1,0:T(8,128)(2,1)}, bf16[128,1024]{1,0:T(8,128)(2,1)}, bf16[128,1024]{1,0:T(8,128)(2,1)}, bf16[128,1024]{1,0:T(8,128)(2,1)}, bf16[8,256,256]{2,1,0:T(8,128)(2,1)}) custom-call(s32[1]{0:T(128)} %bitcast.place, s32[32]{0:T(128)} %spans.3, s32[8]{0:T(128)} %lens.3, bf16[128,4096]{1,0:T(8,128)(2,1)} %refs_0_.1, ...), custom_call_target="tpu_custom_call" | custom-call | flops 12000000000 | bytes 6291456 | tf_op jit(solution)/shard_map/chip_grads/pallas_call | solution.py:182
  44.4 1.6 %collective-permute-start.7 = (bf16[128,1024]{1,0:T(8,128)(2,1)}, bf16[128,1024]{1,0:T(8,128)(2,1)S(1)}, u32[]{:S(2)}, u32[]{:S(2)}) collective-permute-start(bf16[128,1024]{1,0:T(8,128)(2,1)} %get-tuple-element.30), channel_id=1, source_target_pairs={{0,1},{1,0},{2,3},{3,2},{4,5},{5,4},{6,7},{7,6},{8,9},{9,8},{10,11... | collective-permute-start | bytes 786440 | tf_op jit(solution)/shard_map/ppermute | solution.py:40
  46.1 3.0 %all-to-all-done.1.refs_8_ = bf16[8,256,256]{2,1,0:T(8,128)(2,1)S(1)} async-done(((bf16[8,256,256]{2,1,0:T(8,128)(2,1)}), bf16[8,256,256]{2,1,0:T(8,128)(2,1)S(1)}, u32[]{:S(2)}, u32[]{:S(2)}) %all-to-all-start.1) | async-done | bytes 1048608 | tf_op jit(solution)/shard_map/all_to_all | solution.py:45
  49.1 1.0 copy-done
  50.0 9.0 %all-to-all-start.2 = ((bf16[8,256,256]{2,1,0:T(8,128)(2,1)}), bf16[8,256,256]{2,1,0:T(8,128)(2,1)S(1)}, u32[]{:S(2)}, u32[]{:S(2)}) async-start(bf16[8,256,256]{2,1,0:T(8,128)(2,1)} %get-tuple-element.32), calls=%async_computation.2 | async-start | bytes 2097152 | tf_op jit(solution)/shard_map/all_to_all | solution.py:45
  59.0 10.7 %chip_grads.3 = (bf16[128,1024]{1,0:T(8,128)(2,1)}, bf16[128,1024]{1,0:T(8,128)(2,1)}, bf16[128,1024]{1,0:T(8,128)(2,1)}, bf16[128,1024]{1,0:T(8,128)(2,1)}, bf16[8,256,256]{2,1,0:T(8,128)(2,1)}) custom-call(s32[1]{0:T(128)} %bitcast.place, s32[32]{0:T(128)} %spans.3, s32[8]{0:T(128)} %lens.3, bf16[128,4096]{1,0:T(8,128)(2,1)} %refs_0_.1, ...), custom_call_target="tpu_custom_call" | custom-call | flops 12000000000 | bytes 6291456 | tf_op jit(solution)/shard_map/chip_grads/pallas_call | solution.py:182
  70.6 5.5 %all-to-all-done.2 = bf16[8,256,256]{2,1,0:T(8,128)(2,1)S(1)} async-done(((bf16[8,256,256]{2,1,0:T(8,128)(2,1)}), bf16[8,256,256]{2,1,0:T(8,128)(2,1)S(1)}, u32[]{:S(2)}, u32[]{:S(2)}) %all-to-all-start.2) | async-done | bytes 1048608 | tf_op jit(solution)/shard_map/all_to_all | solution.py:45
  76.1 6.7 %all-to-all-start.3 = ((bf16[8,256,256]{2,1,0:T(8,128)(2,1)}), bf16[8,256,256]{2,1,0:T(8,128)(2,1)S(1)}, u32[]{:S(2)}, u32[]{:S(2)}) async-start(bf16[8,256,256]{2,1,0:T(8,128)(2,1)} %get-tuple-element.33), calls=%async_computation.3 | async-start | bytes 2097152 | tf_op jit(solution)/shard_map/all_to_all | solution.py:45
  82.8 2.3 %maximum_select_fusion.1 = bf16[128,4096]{1,0:T(8,128)(2,1)} fusion(bf16[128,1024]{1,0:T(8,128)(2,1)} %collective-permute-done.8, bf16[128,1024]{1,0:T(8,128)(2,1)S(1)} %collective-permute-done.7, bf16[128,1024]{1,0:T(8,128)(2,1)S(1)} %copy-done.5, bf16[128,1024]{1,0:T(8,128)(2,1)S(1)} %copy-done.3, pred[]{:T(512)S(6)} %eq.2), kind=kLoop, calls=%fused_computation.1 | loop fusion | flops 8912896 | bytes 2097153 | tf_op jit(solution)/shard_map/jit(_where)/select_n | solution.py:241
  85.1 1.2 %maximum_select_fusion = bf16[128,4096]{1,0:T(8,128)(2,1)} fusion(bf16[128,1024]{1,0:T(8,128)(2,1)S(1)} %collective-permute-done.6, bf16[128,1024]{1,0:T(8,128)(2,1)S(1)} %collective-permute-done.5, bf16[128,1024]{1,0:T(8,128)(2,1)S(1)} %copy-done.4, bf16[128,1024]{1,0:T(8,128)(2,1)S(1)} %copy-done.2, pred[]{:T(512)S(6)} %eq.2), kind=kLoop, calls=%fused_computation | loop fusion | flops 8912896 | bytes 2097153 | tf_op jit(solution)/shard_map/jit(_where)/select_n | solution.py:241
  86.6 13.2 %all-to-all-done.3 = bf16[8,256,256]{2,1,0:T(8,128)(2,1)S(1)} async-done(((bf16[8,256,256]{2,1,0:T(8,128)(2,1)}), bf16[8,256,256]{2,1,0:T(8,128)(2,1)S(1)}, u32[]{:S(2)}, u32[]{:S(2)}) %all-to-all-start.3) | async-done | bytes 1048608 | tf_op jit(solution)/shard_map/all_to_all | solution.py:45
  99.9 1.3 %collective-permute-start.9 = (bf16[128,512]{1,0:T(8,128)(2,1)S(1)}, bf16[128,512]{1,0:T(8,128)(2,1)S(1)}, u32[]{:S(2)}, u32[]{:S(2)}) collective-permute-start(bf16[128,512]{1,0:T(8,128)(2,1)S(1)} %pad_maximum_fusion.3), channel_id=1, source_target_pairs={{0,1},{1,0},{2,3},{3,2},{4,5},{5,4},{6,7},{7,6},{8,9},{9,8},{10,11... | collective-permute-start | bytes 393224 | tf_op jit(solution)/shard_map/ppermute | solution.py:40
  101.2 1.0 collective-permute-done.9
  102.2 0.7 maximum_select_fusion.3
  102.9 0.7 maximum_select_fusion.2
  (39 shorter events, 2.2 us)
Async XLA Ops:
  1.6 2.9 %copy-start.6 = (bf16[128,4096]{1,0:T(8,128)(2,1)S(1)}, bf16[128,4096]{1,0:T(8,128)(2,1)}, u32[]{:S(2)}) copy-start(bf16[128,4096]{1,0:T(8,128)(2,1)} %refs_0_.1) | copy-start | bytes 3145732
  1.6 1.7 %collective-permute-start = (bf16[128,512]{1,0:T(8,128)(2,1)S(1)}, bf16[128,512]{1,0:T(8,128)(2,1)S(1)}, u32[]{:S(2)}, u32[]{:S(2)}) collective-permute-start(bf16[128,512]{1,0:T(8,128)(2,1)S(1)} %pad_maximum_fusion), channel_id=1, source_target_pairs={{0,1},{1,0},{2,3},{3,2},{4,5},{5,4},{6,7},{7,6},{8,9},{9,8},{10,11... | collective-permute-start | bytes 393224 | tf_op jit(solution)/shard_map/ppermute | solution.py:40
  4.4 29.3 %collective-permute-start.1 = (bf16[128,4096]{1,0:T(8,128)(2,1)S(1)}, bf16[128,4096]{1,0:T(8,128)(2,1)}, u32[]{:S(2)}, u32[]{:S(2)}) collective-permute-start(bf16[128,4096]{1,0:T(8,128)(2,1)S(1)} %copy-done.6), channel_id=1, source_target_pairs={{0,1},{1,0},{2,3},{3,2},{4,5},{5,4},{6,7},{7,6},{8,9},{9,8},{10,11... | collective-permute-start | bytes 3145736 | tf_op jit(solution)/shard_map/ppermute | solution.py:40
  4.8 29.0 %collective-permute-start.2 = (bf16[128,4096]{1,0:T(8,128)(2,1)}, bf16[128,4096]{1,0:T(8,128)(2,1)}, u32[]{:S(2)}, u32[]{:S(2)}) collective-permute-start(bf16[128,4096]{1,0:T(8,128)(2,1)} %refs_1_.1), channel_id=1, source_target_pairs={{0,1},{1,0},{2,3},{3,2},{4,5},{5,4},{6,7},{7,6},{8,9},{9,8},{10,11... | collective-permute-start | bytes 3145736 | tf_op jit(solution)/shard_map/ppermute | solution.py:40
  4.9 28.8 %collective-permute-start.3 = (bf16[128,4096]{1,0:T(8,128)(2,1)}, bf16[128,4096]{1,0:T(8,128)(2,1)}, u32[]{:S(2)}, u32[]{:S(2)}) collective-permute-start(bf16[128,4096]{1,0:T(8,128)(2,1)} %refs_2_.1), channel_id=1, source_target_pairs={{0,1},{1,0},{2,3},{3,2},{4,5},{5,4},{6,7},{7,6},{8,9},{9,8},{10,11... | collective-permute-start | bytes 3145736 | tf_op jit(solution)/shard_map/ppermute | solution.py:40
  5.3 28.5 %collective-permute-start.4 = (bf16[128,4096]{1,0:T(8,128)(2,1)}, bf16[128,4096]{1,0:T(8,128)(2,1)}, u32[]{:S(2)}, u32[]{:S(2)}) collective-permute-start(bf16[128,4096]{1,0:T(8,128)(2,1)} %refs_3_.1), channel_id=1, source_target_pairs={{0,1},{1,0},{2,3},{3,2},{4,5},{5,4},{6,7},{7,6},{8,9},{9,8},{10,11... | collective-permute-start | bytes 3145736 | tf_op jit(solution)/shard_map/ppermute | solution.py:40
  5.4 23.4 %all-to-all-start = ((bf16[8,256,256]{2,1,0:T(8,128)(2,1)}), bf16[8,256,256]{2,1,0:T(8,128)(2,1)S(1)}, u32[]{:S(2)}, u32[]{:S(2)}) async-start(bf16[8,256,256]{2,1,0:T(8,128)(2,1)} %broadcast_in_dim.6), calls=%async_computation | async-start | bytes 2097152 | tf_op jit(solution)/shard_map/all_to_all | solution.py:45
  28.8 1.3 %copy-start.1 = (bf16[8,256,256]{2,1,0:T(8,128)(2,1)}, bf16[8,256,256]{2,1,0:T(8,128)(2,1)S(1)}, u32[]{:S(2)}) copy-start(bf16[8,256,256]{2,1,0:T(8,128)(2,1)S(1)} %all-to-all-done.refs_8_) | copy-start | bytes 3145732
  30.2 18.9 %all-to-all-start.1 = ((bf16[8,256,256]{2,1,0:T(8,128)(2,1)}), bf16[8,256,256]{2,1,0:T(8,128)(2,1)S(1)}, u32[]{:S(2)}, u32[]{:S(2)}) async-start(bf16[8,256,256]{2,1,0:T(8,128)(2,1)} %broadcast_in_dim.7), calls=%async_computation.1 | async-start | bytes 2097152 | tf_op jit(solution)/shard_map/all_to_all | solution.py:45
  44.4 38.3 %collective-permute-start.7 = (bf16[128,1024]{1,0:T(8,128)(2,1)}, bf16[128,1024]{1,0:T(8,128)(2,1)S(1)}, u32[]{:S(2)}, u32[]{:S(2)}) collective-permute-start(bf16[128,1024]{1,0:T(8,128)(2,1)} %get-tuple-element.30), channel_id=1, source_target_pairs={{0,1},{1,0},{2,3},{3,2},{4,5},{5,4},{6,7},{7,6},{8,9},{9,8},{10,11... | collective-permute-start | bytes 786440 | tf_op jit(solution)/shard_map/ppermute | solution.py:40
  49.1 1.0 copy-start
  50.0 26.0 %all-to-all-start.2 = ((bf16[8,256,256]{2,1,0:T(8,128)(2,1)}), bf16[8,256,256]{2,1,0:T(8,128)(2,1)S(1)}, u32[]{:S(2)}, u32[]{:S(2)}) async-start(bf16[8,256,256]{2,1,0:T(8,128)(2,1)} %get-tuple-element.32), calls=%async_computation.2 | async-start | bytes 2097152 | tf_op jit(solution)/shard_map/all_to_all | solution.py:45
  69.7 13.1 %collective-permute-start.8 = (bf16[128,1024]{1,0:T(8,128)(2,1)}, bf16[128,1024]{1,0:T(8,128)(2,1)}, u32[]{:S(2)}, u32[]{:S(2)}) collective-permute-start(bf16[128,1024]{1,0:T(8,128)(2,1)} %get-tuple-element.31), channel_id=1, source_target_pairs={{0,1},{1,0},{2,3},{3,2},{4,5},{5,4},{6,7},{7,6},{8,9},{9,8},{10,11... | collective-permute-start | bytes 786440 | tf_op jit(solution)/shard_map/ppermute | solution.py:40
  70.0 15.1 %collective-permute-start.5 = (bf16[128,1024]{1,0:T(8,128)(2,1)}, bf16[128,1024]{1,0:T(8,128)(2,1)S(1)}, u32[]{:S(2)}, u32[]{:S(2)}) collective-permute-start(bf16[128,1024]{1,0:T(8,128)(2,1)} %get-tuple-element.26), channel_id=1, source_target_pairs={{0,1},{1,0},{2,3},{3,2},{4,5},{5,4},{6,7},{7,6},{8,9},{9,8},{10,11... | collective-permute-start | bytes 786440 | tf_op jit(solution)/shard_map/ppermute | solution.py:40
  70.3 14.9 %collective-permute-start.6 = (bf16[128,1024]{1,0:T(8,128)(2,1)}, bf16[128,1024]{1,0:T(8,128)(2,1)S(1)}, u32[]{:S(2)}, u32[]{:S(2)}) collective-permute-start(bf16[128,1024]{1,0:T(8,128)(2,1)} %get-tuple-element.27), channel_id=1, source_target_pairs={{0,1},{1,0},{2,3},{3,2},{4,5},{5,4},{6,7},{7,6},{8,9},{9,8},{10,11... | collective-permute-start | bytes 786440 | tf_op jit(solution)/shard_map/ppermute | solution.py:40
  76.0 6.7 %copy-start.3 = (bf16[128,1024]{1,0:T(8,128)(2,1)S(1)}, bf16[128,1024]{1,0:T(8,128)(2,1)}, u32[]{:S(2)}) copy-start(bf16[128,1024]{1,0:T(8,128)(2,1)} %get-tuple-element.28) | copy-start | bytes 786436
  76.1 6.7 %copy-start.5 = (bf16[128,1024]{1,0:T(8,128)(2,1)S(1)}, bf16[128,1024]{1,0:T(8,128)(2,1)}, u32[]{:S(2)}) copy-start(bf16[128,1024]{1,0:T(8,128)(2,1)} %get-tuple-element.29) | copy-start | bytes 786436
  76.1 23.7 %all-to-all-start.3 = ((bf16[8,256,256]{2,1,0:T(8,128)(2,1)}), bf16[8,256,256]{2,1,0:T(8,128)(2,1)S(1)}, u32[]{:S(2)}, u32[]{:S(2)}) async-start(bf16[8,256,256]{2,1,0:T(8,128)(2,1)} %get-tuple-element.33), calls=%async_computation.3 | async-start | bytes 2097152 | tf_op jit(solution)/shard_map/all_to_all | solution.py:45
  82.8 2.3 %copy-start.2 = (bf16[128,1024]{1,0:T(8,128)(2,1)S(1)}, bf16[128,1024]{1,0:T(8,128)(2,1)}, u32[]{:S(2)}) copy-start(bf16[128,1024]{1,0:T(8,128)(2,1)} %get-tuple-element.24) | copy-start | bytes 786436
  82.8 2.3 %copy-start.4 = (bf16[128,1024]{1,0:T(8,128)(2,1)S(1)}, bf16[128,1024]{1,0:T(8,128)(2,1)}, u32[]{:S(2)}) copy-start(bf16[128,1024]{1,0:T(8,128)(2,1)} %get-tuple-element.25) | copy-start | bytes 786436
  99.9 2.3 %collective-permute-start.9 = (bf16[128,512]{1,0:T(8,128)(2,1)S(1)}, bf16[128,512]{1,0:T(8,128)(2,1)S(1)}, u32[]{:S(2)}, u32[]{:S(2)}) collective-permute-start(bf16[128,512]{1,0:T(8,128)(2,1)S(1)} %pad_maximum_fusion.3), channel_id=1, source_target_pairs={{0,1},{1,0},{2,3},{3,2},{4,5},{5,4},{6,7},{7,6},{8,9},{9,8},{10,11... | collective-permute-start | bytes 393224 | tf_op jit(solution)/shard_map/ppermute | solution.py:40
